TPU v7x, 32 devices: a whole 2x2x4 slice. The times are simulated.
32 devices in a mesh: section: 2 (over x), seq: 4 (over z), fsdp: 4 (over y, core).
Axes of the slice: x: 2, y: 2, z: 4, core: 2. Of those that a mesh axis runs over, the one named last changes fastest.
Arguments:
- inputs: bfloat16 [2, 4, 1024, 768], P(None, 'fsdp', 'seq'), may hold values from -6 to 6
- cotangent: bfloat16 [2, 4, 1024, 768], P(None, 'fsdp', 'seq'), may hold values from -6 to 6
- w_qkv: bfloat16 [2, 768, 2304], P('section', 'fsdp'), may hold values from -0.21875 to 0.21875
- w_attn_out: bfloat16 [2, 768, 768], P('section', 'fsdp'), may hold values from -2.5 to 2.5
- w_in: bfloat16 [2, 768, 2304], P('section', 'fsdp'), may hold values from -0.21875 to 0.21875
- w_ff_out: bfloat16 [2, 1152, 768], P('section', 'fsdp'), may hold values from -0.1875 to 0.1875
- ln_attn: bfloat16 [2, 768], P('section', 'fsdp'), may hold values from 0.5 to 1.5
- ln_ff: bfloat16 [2, 768], P('section', 'fsdp'), may hold values from 0.5 to 1.5
Outputs:
- layer_out: bfloat16 [2, 2, 4, 1024, 768], P('section', None, 'fsdp', 'seq')
- in_grad: float32 [2, 2, 4, 1024, 768], P('section', None, 'fsdp', 'seq')
- g_qkv: float32 [2, 768, 2304], P('section', 'fsdp')
- g_attn_out: float32 [2, 768, 768], P('section', 'fsdp')
- g_in: float32 [2, 768, 2304], P('section', 'fsdp')
- g_ff_out: float32 [2, 1152, 768], P('section', 'fsdp')
- g_ln_attn: float32 [2, 768], P('section', 'fsdp')
- g_ln_ff: float32 [2, 768], P('section', 'fsdp')
All inputs are finite; a program needn't handle non-finite values.
Results may differ from a plain program's by a relative error of at most 0.023.
Values may be sent and summed in bfloat16 or wider, within the bound.
A program may use at most 128 MiB of HBM per device.

v0:
```python
import jax
import jax.numpy as jnp
from jax import lax
from jax.sharding import PartitionSpec as P

D = 768
HEADS = 12
HEAD_DIM = 64
FF = 1152
HALF = 64


def padded(cells, sides, width):
    for axis, dim in sides:
        count = lax.axis_size(axis)
        ends = count - 1
        head = lax.slice_in_dim(cells, 0, width, axis=dim)
        tail = lax.slice_in_dim(cells, cells.shape[dim] - width, cells.shape[dim], axis=dim)
        cells = jnp.concatenate(
            [
                lax.ppermute(tail, axis, [(i, (i + 1) % count) for i in range(ends)]),
                cells,
                lax.ppermute(head, axis, [((i + 1) % count, i) for i in range(ends)]),
            ],
            axis=dim,
        )
    return cells


def from_behind(x, axis, by):
    count = lax.axis_size(axis)
    pairs = [(i, i + by) for i in range(count) if 0 <= i + by < count]
    return lax.ppermute(x, axis, pairs)


def as_sent(x):
    return jax.tree.map(lambda a: a.astype(jnp.bfloat16) if a.dtype == jnp.float32 else a, x)


def layer_norm(values, gain):
    centre = values - jnp.mean(values, axis=-1, keepdims=True)
    spread = jnp.mean(centre * centre, axis=-1, keepdims=True)
    return centre * lax.rsqrt(spread + 1e-05) * gain


def gated_unit(gate_up):
    return jax.nn.gelu(gate_up[:, :FF], approximate=False) * gate_up[:, FF:]


def attention_probs(queries, keys_padded, allowed):
    rows = queries.shape[0]
    query_heads = queries.reshape(rows, HEADS, HEAD_DIM)
    key_heads = keys_padded[:, :D].reshape(-1, HEADS, HEAD_DIM)
    scores = jnp.einsum(
        "qhd,khd->hqk", query_heads, key_heads, preferred_element_type=jnp.float32
    ) * HEAD_DIM ** (-0.5)
    scores = jnp.where(allowed[None], scores, -1e30)
    top_score = jnp.max(scores, axis=-1, keepdims=True)
    expo = jnp.exp(scores - top_score)
    return expo / jnp.sum(expo, axis=-1, keepdims=True)


def body(inputs, cotangent, w_qkv, w_attn_out, w_in, w_ff_out, ln_attn, ln_ff):
    section_idx = lax.axis_index("section")
    seq_idx = lax.axis_index("seq")
    seq_count = lax.axis_size("seq")
    micro_count = inputs.shape[0]
    block_rows = inputs.shape[2]
    padded_rows = block_rows + 2 * HALF
    gathered = (
        lax.all_gather(w_qkv, "fsdp", axis=1, tiled=True),
        lax.all_gather(w_attn_out, "fsdp", axis=1, tiled=True),
        lax.all_gather(w_in, "fsdp", axis=1, tiled=True),
        lax.all_gather(w_ff_out, "fsdp", axis=1, tiled=True),
        lax.all_gather(ln_attn, "fsdp", axis=1, tiled=True),
        lax.all_gather(ln_ff, "fsdp", axis=1, tiled=True),
    )
    mat_qkv = gathered[0][0]
    mat_out = gathered[1][0]
    mat_in = gathered[2][0]
    mat_ff = gathered[3][0]
    gain_attn = gathered[4][0].astype(jnp.float32)
    gain_ff = gathered[5][0].astype(jnp.float32)
    query_pos = jnp.arange(block_rows, dtype=jnp.int32)[:, None]
    key_pos = jnp.arange(padded_rows, dtype=jnp.int32)[None, :] - HALF
    global_key = seq_idx * block_rows + key_pos
    allowed = (
        (jnp.abs(key_pos - query_pos) <= HALF)
        & (global_key >= 0)
        & (global_key < seq_count * block_rows)
    )
    zero_rows = jnp.zeros((block_rows, D), jnp.bfloat16)
    kept_list = []
    out_list = []
    sent_rows = zero_rows
    for slot_idx in range(micro_count + 1):
        if slot_idx == 0:
            received = zero_rows
        else:
            received = from_behind(sent_rows, "section", 1)
        own_rows = inputs[slot_idx, 0] if slot_idx < micro_count else zero_rows
        layer_in = jnp.where(section_idx == 0, own_rows, received)
        forward_in_float = layer_in.astype(jnp.float32)
        forward_normed = layer_norm(forward_in_float, gain_attn).astype(jnp.bfloat16)
        projected = jnp.dot(forward_normed, mat_qkv, preferred_element_type=jnp.float32).astype(
            jnp.bfloat16
        )
        forward_queries = projected[:, :D]
        forward_keys_padded = padded(projected[:, D:], (("seq", 0),), HALF)
        forward_probs = attention_probs(forward_queries, forward_keys_padded, allowed)
        forward_value_heads = forward_keys_padded[:, D:].reshape(padded_rows, HEADS, HEAD_DIM)
        forward_attended = jnp.einsum(
            "hqk,khd->qhd",
            forward_probs.astype(jnp.bfloat16),
            forward_value_heads,
            preferred_element_type=jnp.float32,
        )
        forward_attended = forward_attended.reshape(block_rows, D).astype(jnp.bfloat16)
        forward_hidden_in = forward_in_float + jnp.dot(
            forward_attended, mat_out, preferred_element_type=jnp.float32
        )
        forward_normed_ff = layer_norm(forward_hidden_in, gain_ff).astype(jnp.bfloat16)
        forward_gate_up = jnp.dot(forward_normed_ff, mat_in, preferred_element_type=jnp.float32)
        forward_hidden = gated_unit(forward_gate_up).astype(jnp.bfloat16)
        result = forward_hidden_in + jnp.dot(
            forward_hidden, mat_ff, preferred_element_type=jnp.float32
        )
        result, kept = (
            result,
            (
                layer_in,
                forward_queries,
                forward_keys_padded,
                forward_attended,
                forward_hidden_in,
                forward_gate_up,
            ),
        )
        sent_rows = result.astype(jnp.bfloat16)
        kept_list.append(kept)
        out_list.append(sent_rows)
    kept_stack = jax.tree.map(lambda *pieces: jnp.stack(pieces), *kept_list)
    out_stack = jnp.stack(out_list)
    gain_totals = (jnp.zeros((D,), jnp.float32), jnp.zeros((D,), jnp.float32))
    factor_list = []
    grad_list = []
    back_rows = zero_rows
    for slot_idx in range(micro_count + 1):
        if slot_idx == 0:
            received_grad = zero_rows
        else:
            received_grad = from_behind(back_rows, "section", -1)
        if slot_idx < micro_count:
            own_grad = cotangent[slot_idx, 0].astype(jnp.float32)
        else:
            own_grad = jnp.zeros((block_rows, D), jnp.float32)
        grad_out = jnp.where(section_idx == 1, own_grad, received_grad.astype(jnp.float32))
        kept_slot = jnp.clip(slot_idx + 2 * section_idx - 1, 0, micro_count)
        kept = jax.tree.map(
            lambda stacked: lax.dynamic_index_in_dim(stacked, kept_slot, 0, keepdims=False),
            kept_stack,
        )
        backward_layer_in, queries, keys_padded, attended, hidden_in, gate_up = kept
        in_float = backward_layer_in.astype(jnp.float32)
        normed, norm_back = jax.vjp(layer_norm, in_float, gain_attn)
        normed_b = normed.astype(jnp.bfloat16)
        normed_ff, norm_ff_back = jax.vjp(layer_norm, hidden_in, gain_ff)
        normed_ff_b = normed_ff.astype(jnp.bfloat16)
        hidden, gated_back = jax.vjp(gated_unit, gate_up)
        hidden_b = hidden.astype(jnp.bfloat16)
        grad_ff = grad_out.astype(jnp.bfloat16)
        grad_hidden = jnp.einsum("td,fd->tf", grad_ff, mat_ff, preferred_element_type=jnp.float32)
        grad_gate_up = gated_back(grad_hidden)[0].astype(jnp.bfloat16)
        grad_normed_ff = jnp.einsum(
            "tf,cf->tc", grad_gate_up, mat_in, preferred_element_type=jnp.float32
        )
        grad_h_norm, grad_gain_ff = norm_ff_back(grad_normed_ff)
        grad_hidden_in = grad_out + grad_h_norm
        grad_attn = grad_hidden_in.astype(jnp.bfloat16)
        grad_attended = jnp.einsum(
            "td,cd->tc", grad_attn, mat_out, preferred_element_type=jnp.float32
        ).astype(jnp.bfloat16)
        probs = attention_probs(queries, keys_padded, allowed)
        probs_b = probs.astype(jnp.bfloat16)
        query_heads = queries.reshape(block_rows, HEADS, HEAD_DIM)
        key_heads = keys_padded[:, :D].reshape(padded_rows, HEADS, HEAD_DIM)
        value_heads = keys_padded[:, D:].reshape(padded_rows, HEADS, HEAD_DIM)
        grad_heads = grad_attended.reshape(block_rows, HEADS, HEAD_DIM)
        grad_probs = jnp.einsum(
            "qhd,khd->hqk", grad_heads, value_heads, preferred_element_type=jnp.float32
        )
        grad_values = jnp.einsum(
            "hqk,qhd->khd", probs_b, grad_heads, preferred_element_type=jnp.float32
        )
        grad_scores = probs * (grad_probs - jnp.sum(probs * grad_probs, axis=-1, keepdims=True))
        grad_scores = grad_scores.astype(jnp.bfloat16)
        scale = HEAD_DIM ** (-0.5)
        grad_queries = scale * jnp.einsum(
            "hqk,khd->qhd", grad_scores, key_heads, preferred_element_type=jnp.float32
        )
        grad_keys = scale * jnp.einsum(
            "hqk,qhd->khd", grad_scores, query_heads, preferred_element_type=jnp.float32
        )
        grad_kv_pad = jnp.concatenate(
            [grad_keys.reshape(padded_rows, D), grad_values.reshape(padded_rows, D)], axis=1
        )
        rims = jnp.concatenate([grad_kv_pad[:HALF], grad_kv_pad[block_rows + HALF :]], axis=0)
        arrived = padded(rims.astype(jnp.bfloat16), (("seq", 0),), HALF).astype(rims.dtype)
        grad_kv = grad_kv_pad[HALF : HALF + block_rows]
        grad_kv = grad_kv + jnp.pad(arrived[:HALF], ((0, block_rows - HALF), (0, 0)))
        grad_kv = grad_kv + jnp.pad(arrived[3 * HALF :], ((block_rows - HALF, 0), (0, 0)))
        grad_proj = jnp.concatenate([grad_queries.reshape(block_rows, D), grad_kv], axis=1).astype(
            jnp.bfloat16
        )
        grad_normed = jnp.einsum(
            "te,ce->tc", grad_proj, mat_qkv, preferred_element_type=jnp.float32
        )
        grad_in_norm, grad_gain_attn = norm_back(grad_normed)
        grad_in = grad_hidden_in + grad_in_norm
        factors = (
            normed_b,
            grad_proj,
            attended,
            grad_attn,
            normed_ff_b,
            grad_gate_up,
            hidden_b,
            grad_ff,
        )
        grad_in, factors, gain_terms = (grad_in, factors, (grad_gain_attn, grad_gain_ff))
        gain_totals = (gain_totals[0] + gain_terms[0], gain_totals[1] + gain_terms[1])
        factor_list.append(factors)
        back_rows = grad_in.astype(jnp.bfloat16)
        grad_list.append(jnp.where(section_idx == 1, back_rows.astype(jnp.float32), grad_in))
    grad_stack = jnp.stack(grad_list)
    factor_all = jax.tree.map(lambda *pieces: jnp.concatenate(pieces, axis=0), *factor_list)
    (
        normed_all,
        grad_proj_all,
        attended_all,
        grad_attn_all,
        normed_ff_all,
        grad_gate_all,
        hidden_all,
        grad_ff_all,
    ) = factor_all
    grad_mat_qkv = jnp.einsum(
        "tc,te->ce", normed_all, grad_proj_all, preferred_element_type=jnp.float32
    )
    grad_mat_out = jnp.einsum(
        "tc,td->cd", attended_all, grad_attn_all, preferred_element_type=jnp.float32
    )
    grad_mat_in = jnp.einsum(
        "tc,tf->cf", normed_ff_all, grad_gate_all, preferred_element_type=jnp.float32
    )
    grad_mat_ff = jnp.einsum(
        "tf,td->fd", hidden_all, grad_ff_all, preferred_element_type=jnp.float32
    )
    totals = (grad_mat_qkv, grad_mat_out, grad_mat_in, grad_mat_ff, gain_totals[0], gain_totals[1])
    layer_out = lax.dynamic_slice_in_dim(out_stack, section_idx, micro_count, 0).reshape(
        1, micro_count, 1, block_rows, D
    )
    in_grad = lax.dynamic_slice_in_dim(grad_stack, 1 - section_idx, micro_count, 0).reshape(
        1, micro_count, 1, block_rows, D
    )
    leading = tuple((total[None] for total in totals))
    owned = jax.tree.map(
        lambda part: part.astype(jnp.float32),
        lax.psum_scatter(as_sent(leading), "fsdp", scatter_dimension=1, tiled=True),
    )
    summed = jax.tree.map(lambda part: part.astype(jnp.float32), lax.psum(as_sent(owned), "seq"))
    return (layer_out, in_grad, summed[0], summed[1], summed[2], summed[3], summed[4], summed[5])


def solution(mesh):
    placed = (
        P(None, "fsdp", "seq", None),
        P(None, "fsdp", "seq", None),
        P("section", "fsdp", None),
        P("section", "fsdp", None),
        P("section", "fsdp", None),
        P("section", "fsdp", None),
        P("section", "fsdp"),
        P("section", "fsdp"),
    )
    return jax.shard_map(
        body,
        mesh=mesh,
        in_specs=placed,
        out_specs=(
            P("section", None, "fsdp", "seq", None),
            P("section", None, "fsdp", "seq", None),
            P("section", "fsdp", None),
            P("section", "fsdp", None),
            P("section", "fsdp", None),
            P("section", "fsdp", None),
            P("section", "fsdp"),
            P("section", "fsdp"),
        ),
        check_vma=False,
    )
```

profile of v0, /device:TPU:0, one launch (start us, length us, event | category | flops | bytes accessed | tf_op | source)
XLA Modules:
  0.0 686.8 jit_solution(50054206184659114)
XLA Ops:
  11.8 8.3 %all-reduce.11 = (bf16[768]{0:T(1024)(128)(2,1)S(1)}, bf16[768]{0:T(1024)(128)(2,1)S(1)}) all-reduce(bf16[768]{0:T(1024)(128)(2,1)S(1)} %dynamic-update-slice, bf16[768]{0:T(1024)(128)(2,1)S(1)} %dynamic-update-slice.1), channel_id=1, replica_groups=mesh['section'=2,'seq'=4,'fsdp'=4] {'fsdp'}, use_global_device_ids=true, to_apply=%add.9 | all-reduce | flops 1536 | bytes 6144
  21.4 21.7 %all-gather.5.cloned.1.call-done = bf16[1,768,2304]{2,1,0:T(8,128)(2,1)} async-done(((bf16[1,192,2304]{2,1,0:T(8,128)(2,1)}), bf16[1,768,2304]{2,1,0:T(8,128)(2,1)}) %all-gather.5.cloned.1.call-update) | async-done | bytes 3538960 | tf_op jit(solution)/shard_map/all_gather | solution.py:71
  47.6 4.6 collective-permute-start
  67.9 26.6 %all-gather.9.cloned.1.call-done = bf16[1,768,2304]{2,1,0:T(8,128)(2,1)} async-done(((bf16[1,192,2304]{2,1,0:T(8,128)(2,1)}), bf16[1,768,2304]{2,1,0:T(8,128)(2,1)}) %all-gather.9.cloned.1.call-update) | async-done | bytes 3538960 | tf_op jit(solution)/shard_map/all_gather | solution.py:73
  97.7 19.1 %all-gather.11.cloned.1.call-done = bf16[1,1152,768]{2,1,0:T(8,128)(2,1)} async-done(((bf16[1,288,768]{2,1,0:T(8,128)(2,1)}), bf16[1,1152,768]{2,1,0:T(8,128)(2,1)}) %all-gather.11.cloned.1.call-update) | async-done | bytes 1769488 | tf_op jit(solution)/shard_map/all_gather | solution.py:74
  116.7 4.7 fusion.133
  125.2 8.5 %collective-permute-done.2 = bf16[256,768]{1,0:T(8,128)(2,1)S(1)} collective-permute-done((bf16[256,768]{1,0:T(8,128)(2,1)S(1)}, bf16[256,768]{1,0:T(8,128)(2,1)S(1)}, u32[]{:S(2)}, u32[]{:S(2)}) %collective-permute-start.2) | collective-permute-done | bytes 393248 | tf_op jit(solution)/shard_map/ppermute | solution.py:33
  136.6 4.6 collective-permute-start.3
  157.6 3.9 fusion.130
  161.6 5.1 collective-permute-start.5
  168.5 4.3 collective-permute-done.5
  180.4 5.9 collective-permute-start.6
  204.7 5.6 fusion.581
  216.3 8.6 %pad_maximum_fusion.1 = bf16[3,384,1536]{2,1,0:T(8,128)(2,1)S(1)} fusion(bf16[1,384,1536]{2,1,0:T(8,128)(2,1)S(1)} %copy-done.39, bf16[1,384,1536]{2,1,0:T(8,128)(2,1)S(1)} %copy-done.38, bf16[1,384,1536]{2,1,0:T(8,128)(2,1)S(1)} %copy-done.37), kind=kLoop, calls=%fused_computation.41 | loop fusion | flops 3538944 | bytes 7077888 | tf_op jit(solution)/shard_map/stack | solution.py:142
  253.9 5.6 fusion.583
  271.7 5.3 collective-permute-start.8
  285.9 4.7 multiply_convert_fusion.3
  290.6 5.7 fusion.584
  310.4 10.8 %collective-permute-done.10 = bf16[256,768]{1,0:T(8,128)(2,1)S(1)} collective-permute-done((bf16[256,768]{1,0:T(8,128)(2,1)S(1)}, bf16[256,768]{1,0:T(8,128)(2,1)S(1)}, u32[]{:S(2)}, u32[]{:S(2)}) %collective-permute-start.10) | collective-permute-done | bytes 393248 | tf_op jit(solution)/shard_map/ppermute | solution.py:33
  342.0 4.6 collective-permute-start.11
  363.1 7.3 %collective-permute-done.13 = bf16[256,768]{1,0:T(8,128)(2,1)S(1)} collective-permute-done((bf16[256,768]{1,0:T(8,128)(2,1)S(1)}, bf16[256,768]{1,0:T(8,128)(2,1)S(1)}, u32[]{:S(2)}, u32[]{:S(2)}) %collective-permute-start.13) | collective-permute-done | bytes 393248 | tf_op jit(solution)/shard_map/ppermute | solution.py:33
  380.9 4.4 fusion.51
  387.2 6.5 fusion.7
  409.2 5.1 collective-permute-start.14
  426.2 13.0 %fusion.6 = bf16[1,768,2304]{2,1,0:T(8,128)(2,1)} fusion(bf16[256,1536]{0,1:T(8,128)(2,1)S(1)} %fusion.105, bf16[256,768]{0,1:T(8,128)(2,1)S(1)} %bitcast.500, bf16[256,1536]{0,1:T(8,128)(2,1)S(1)} %copy-done.82, bf16[256,768]{0,1:T(8,128)(2,1)S(1)} %bitcast.498, bf16[256,1536]{0,1:T(8,128)(2,1)S(1)} %copy-done.80, bf16[256,768]{0,1:T(8,128)(2,1)S(1)} %bitcast.494, ...), kind=kOutput, calls=%fused_computation.30 | convolution fusion | flops 2744451072 | bytes 8257536 | tf_op jit(solution)/shard_map/tc,te->ce/dot_general | solution.py:247
  442.1 39.7 %reduce-scatter.15.cloned.1.call-done = bf16[1,192,2304]{2,1,0:T(8,128)(2,1)} async-done(((bf16[1,768,2304]{2,1,0:T(8,128)(2,1)}), bf16[1,192,2304]{2,1,0:T(8,128)(2,1)}) %reduce-scatter.15.cloned.1.call-update) | async-done | bytes 884752 | tf_op jit(solution)/shard_map/reduce_scatter | solution.py:269
  481.8 43.2 %reduce-scatter.11.cloned.1.call-done = bf16[1,192,2304]{2,1,0:T(8,128)(2,1)} async-done(((bf16[1,768,2304]{2,1,0:T(8,128)(2,1)}), bf16[1,192,2304]{2,1,0:T(8,128)(2,1)}) %reduce-scatter.11.cloned.1.call-update) | async-done | bytes 884752 | tf_op jit(solution)/shard_map/reduce_scatter | solution.py:269
  526.7 4.9 fusion.139
  534.1 13.1 %reduce-scatter.21.cloned.1.call-done = bf16[192,1]{1,0:T(8,128)(2,1)} async-done(((bf16[768,1]{1,0:T(8,128)(2,1)}), bf16[192,1]{1,0:T(8,128)(2,1)}) %reduce-scatter.21.cloned.1.call-update) | async-done | bytes 400
  550.9 18.9 %reduce-scatter.19.cloned.1.call-done = bf16[192,1]{1,0:T(8,128)(2,1)} async-done(((bf16[768,1]{1,0:T(8,128)(2,1)}), bf16[192,1]{1,0:T(8,128)(2,1)}) %reduce-scatter.19.cloned.1.call-update) | async-done | bytes 400
  570.7 11.9 %all-reduce.12 = (bf16[1,192]{1,0:T(2,128)(2,1)S(1)}, bf16[1,192]{1,0:T(2,128)(2,1)S(1)}) all-reduce(bf16[1,192]{1,0:T(2,128)(2,1)S(1)} %copy.74, bf16[1,192]{1,0:T(2,128)(2,1)S(1)} %copy.76), channel_id=1, replica_groups=mesh['section'=2,'seq'=4,'fsdp'=4] {'seq'}, use_global_device_ids=true, to_apply=%region_63.64 | all-reduce | flops 384 | bytes 1536 | tf_op jit(solution)/shard_map/psum | solution.py:271
  583.7 90.4 %all-reduce.16.cloned.1.call-done = (bf16[1,192,2304]{2,1,0:T(8,128)(2,1)}, bf16[1,192,768]{2,1,0:T(8,128)(2,1)}, bf16[1,192,2304]{2,1,0:T(8,128)(2,1)}, bf16[1,288,768]{2,1,0:T(8,128)(2,1)}) async-done(((bf16[1,192,2304]{2,1,0:T(8,128)(2,1)}, bf16[1,192,768]{2,1,0:T(8,128)(2,1)}, bf16[1,192,2304]{2,1,0:T(8,128)(2,1)}, bf16[1,288,768]{2,1,0:T(8,128)(2,1)}), (bf16[1,192,2304]{2,1,0:T(8,128)(2,1)}, ...) | async-done | bytes 2506768 | tf_op jit(solution)/shard_map/psum | solution.py:271
  (556 shorter events, 243.3 us)
Async XLA Ops:
  7.2 35.9 %all-gather.5.cloned.1.call-start = ((), (), s32[]{:S(2)}) async-start(), calls=%async_computation.6 | async-start | bytes 4423680 | tf_op jit(solution)/shard_map/all_gather | solution.py:71
  7.9 57.8 %all-gather.7.cloned.1.call-start = ((), (), s32[]{:S(2)}) async-start(), calls=%async_computation.7 | async-start | bytes 1474560 | tf_op jit(solution)/shard_map/all_gather | solution.py:72
  8.7 85.8 %all-gather.9.cloned.1.call-start = ((), (), s32[]{:S(2)}) async-start(), calls=%async_computation.8 | async-start | bytes 4423680 | tf_op jit(solution)/shard_map/all_gather | solution.py:73
  9.4 107.3 %all-gather.11.cloned.1.call-start = ((), (), s32[]{:S(2)}) async-start(), calls=%async_computation.9 | async-start | bytes 2211840 | tf_op jit(solution)/shard_map/all_gather | solution.py:74
  10.0 432.1 %reduce-scatter.13.cloned.1.call-start = ((), (), s32[]{:S(2)}) async-start(), calls=%async_computation.11 | async-start | bytes 1474560 | tf_op jit(solution)/shard_map/reduce_scatter | solution.py:269
  46.3 8.9 %collective-permute-start.1 = (bf16[64,1536]{1,0:T(8,128)(2,1)S(1)}, bf16[64,1536]{1,0:T(8,128)(2,1)S(1)}, u32[]{:S(2)}, u32[]{:S(2)}) collective-permute-start(bf16[64,1536]{1,0:T(8,128)(2,1)S(1)} %get-tuple-element.122), channel_id=1, source_target_pairs={{4,0},{8,4},{12,8},{5,1},{9,5},{13,9},{6,2},{10,6},{14,10},{7,3},{... | collective-permute-start | bytes 589832 | tf_op jit(solution)/shard_map/ppermute | solution.py:23
  47.6 8.8 %collective-permute-start = (bf16[64,1536]{1,0:T(8,128)(2,1)S(1)}, bf16[64,1536]{1,0:T(8,128)(2,1)S(1)}, u32[]{:S(2)}, u32[]{:S(2)}) collective-permute-start(bf16[64,1536]{1,0:T(8,128)(2,1)S(1)} %get-tuple-element.121), channel_id=1, source_target_pairs={{0,4},{4,8},{8,12},{1,5},{5,9},{9,13},{2,6},{6,10},{10,14},{3,7},{... | collective-permute-start | bytes 589832 | tf_op jit(solution)/shard_map/ppermute | solution.py:21
  67.7 49.0 %copy-start.31 = (f32[256,768]{1,0:T(8,128)}, f32[256,768]{1,0:T(8,128)S(1)}, u32[]{:S(2)}) copy-start(f32[256,768]{1,0:T(8,128)S(1)} %get-tuple-element.130) | copy-start | bytes 2359300
  97.7 23.8 %copy-start.18 = (f32[256,2304]{1,0:T(8,128)}, f32[256,2304]{1,0:T(8,128)S(1)}, u32[]{:S(2)}) copy-start(f32[256,2304]{1,0:T(8,128)S(1)} %fusion.40) | copy-start | bytes 7077892
  116.7 17.4 %copy-start.139 = (bf16[1,768,2304]{2,1,0:T(8,128)(2,1)S(1)}, bf16[1,768,2304]{2,1,0:T(8,128)(2,1)}, u32[]{:S(2)}) copy-start(bf16[1,768,2304]{2,1,0:T(8,128)(2,1)} %all-gather.5.cloned.1.call-done) | copy-start | bytes 10616836
  121.5 12.1 %collective-permute-start.2 = (bf16[256,768]{1,0:T(8,128)(2,1)S(1)}, bf16[256,768]{1,0:T(8,128)(2,1)S(1)}, u32[]{:S(2)}, u32[]{:S(2)}) collective-permute-start(bf16[256,768]{1,0:T(8,128)(2,1)S(1)} %fusion.133), channel_id=1, source_target_pairs={{0,16},{1,17},{2,18},{3,19},{4,20},{5,21},{6,22},{7,23},{8,24},{9,... | collective-permute-start | bytes 1179656 | tf_op jit(solution)/shard_map/ppermute | solution.py:33
  135.3 8.1 %collective-permute-start.4 = (bf16[64,1536]{1,0:T(8,128)(2,1)S(1)}, bf16[64,1536]{1,0:T(8,128)(2,1)S(1)}, u32[]{:S(2)}, u32[]{:S(2)}) collective-permute-start(bf16[64,1536]{1,0:T(8,128)(2,1)S(1)} %get-tuple-element.118), channel_id=1, source_target_pairs={{4,0},{8,4},{12,8},{5,1},{9,5},{13,9},{6,2},{10,6},{14,10},{7,3},{... | collective-permute-start | bytes 589832 | tf_op jit(solution)/shard_map/ppermute | solution.py:23
  136.6 8.0 %collective-permute-start.3 = (bf16[64,1536]{1,0:T(8,128)(2,1)S(1)}, bf16[64,1536]{1,0:T(8,128)(2,1)S(1)}, u32[]{:S(2)}, u32[]{:S(2)}) collective-permute-start(bf16[64,1536]{1,0:T(8,128)(2,1)S(1)} %get-tuple-element.117), channel_id=1, source_target_pairs={{0,4},{4,8},{8,12},{1,5},{5,9},{9,13},{2,6},{6,10},{10,14},{3,7},{... | collective-permute-start | bytes 589832 | tf_op jit(solution)/shard_map/ppermute | solution.py:21
  161.6 11.2 %collective-permute-start.5 = (bf16[256,768]{1,0:T(8,128)(2,1)}, bf16[256,768]{1,0:T(8,128)(2,1)}, u32[]{:S(2)}, u32[]{:S(2)}) collective-permute-start(bf16[256,768]{1,0:T(8,128)(2,1)} %fusion.130), channel_id=1, source_target_pairs={{0,16},{1,17},{2,18},{3,19},{4,20},{5,21},{6,22},{7,23},{8,24},{9,... | collective-permute-start | bytes 1179656 | tf_op jit(solution)/shard_map/ppermute | solution.py:33
  179.1 17.8 %collective-permute-start.7 = (bf16[64,1536]{1,0:T(8,128)(2,1)}, bf16[64,1536]{1,0:T(8,128)(2,1)}, u32[]{:S(2)}, u32[]{:S(2)}) collective-permute-start(bf16[64,1536]{1,0:T(8,128)(2,1)} %get-tuple-element.114), channel_id=1, source_target_pairs={{4,0},{8,4},{12,8},{5,1},{9,5},{13,9},{6,2},{10,6},{14,10},{7,3},{... | collective-permute-start | bytes 589832 | tf_op jit(solution)/shard_map/ppermute | solution.py:23
  180.4 16.5 %collective-permute-start.6 = (bf16[64,1536]{1,0:T(8,128)(2,1)}, bf16[64,1536]{1,0:T(8,128)(2,1)}, u32[]{:S(2)}, u32[]{:S(2)}) collective-permute-start(bf16[64,1536]{1,0:T(8,128)(2,1)} %get-tuple-element.113), channel_id=1, source_target_pairs={{0,4},{4,8},{8,12},{1,5},{5,9},{9,13},{2,6},{6,10},{10,14},{3,7},{... | collective-permute-start | bytes 589832 | tf_op jit(solution)/shard_map/ppermute | solution.py:21
  190.4 112.4 %copy-start.107 = (f32[256]{0:T(256)}, f32[256]{0:T(256)S(1)}, u32[]{:S(2)}) copy-start(f32[256]{0:T(256)S(1)} %broadcast_multiply_fusion.4) | copy-start | bytes 3076
  270.4 26.6 %collective-permute-start.9 = (bf16[64,1536]{0,1:T(8,128)(2,1)}, bf16[64,1536]{0,1:T(8,128)(2,1)}, u32[]{:S(2)}, u32[]{:S(2)}) collective-permute-start(bf16[64,1536]{0,1:T(8,128)(2,1)} %get-tuple-element.96), channel_id=1, source_target_pairs={{4,0},{8,4},{12,8},{5,1},{9,5},{13,9},{6,2},{10,6},{14,10},{7,3},{... | collective-permute-start | bytes 589832 | tf_op jit(solution)/shard_map/ppermute | solution.py:23
  271.7 25.3 %collective-permute-start.8 = (bf16[64,1536]{0,1:T(8,128)(2,1)}, bf16[64,1536]{0,1:T(8,128)(2,1)}, u32[]{:S(2)}, u32[]{:S(2)}) collective-permute-start(bf16[64,1536]{0,1:T(8,128)(2,1)} %get-tuple-element.95), channel_id=1, source_target_pairs={{0,4},{4,8},{8,12},{1,5},{5,9},{9,13},{2,6},{6,10},{10,14},{3,7},{... | collective-permute-start | bytes 589832 | tf_op jit(solution)/shard_map/ppermute | solution.py:21
  303.1 18.2 %copy-start.145 = (bf16[1,1152,768]{2,1,0:T(8,128)(2,1)S(1)}, bf16[1,1152,768]{2,1,0:T(8,128)(2,1)}, u32[]{:S(2)}) copy-start(bf16[1,1152,768]{2,1,0:T(8,128)(2,1)} %all-gather.11.cloned.1.call-done) | copy-start | bytes 5308420
  307.9 13.3 %collective-permute-start.10 = (bf16[256,768]{1,0:T(8,128)(2,1)S(1)}, bf16[256,768]{1,0:T(8,128)(2,1)S(1)}, u32[]{:S(2)}, u32[]{:S(2)}) collective-permute-start(bf16[256,768]{1,0:T(8,128)(2,1)S(1)} %get-tuple-element.56), channel_id=1, source_target_pairs={{16,0},{17,1},{18,2},{19,3},{20,4},{21,5},{22,6},{23,7},{24,8},{25... | collective-permute-start | bytes 1179656 | tf_op jit(solution)/shard_map/ppermute | solution.py:33
  340.7 9.7 %collective-permute-start.12 = (bf16[64,1536]{0,1:T(8,128)(2,1)S(1)}, bf16[64,1536]{0,1:T(8,128)(2,1)S(1)}, u32[]{:S(2)}, u32[]{:S(2)}) collective-permute-start(bf16[64,1536]{0,1:T(8,128)(2,1)S(1)} %get-tuple-element.92), channel_id=1, source_target_pairs={{4,0},{8,4},{12,8},{5,1},{9,5},{13,9},{6,2},{10,6},{14,10},{7,3},{... | collective-permute-start | bytes 589832 | tf_op jit(solution)/shard_map/ppermute | solution.py:23
  342.0 9.8 %collective-permute-start.11 = (bf16[64,1536]{0,1:T(8,128)(2,1)S(1)}, bf16[64,1536]{0,1:T(8,128)(2,1)S(1)}, u32[]{:S(2)}, u32[]{:S(2)}) collective-permute-start(bf16[64,1536]{0,1:T(8,128)(2,1)S(1)} %get-tuple-element.91), channel_id=1, source_target_pairs={{0,4},{4,8},{8,12},{1,5},{5,9},{9,13},{2,6},{6,10},{10,14},{3,7},{... | collective-permute-start | bytes 589832 | tf_op jit(solution)/shard_map/ppermute | solution.py:21
  360.5 9.8 %collective-permute-start.13 = (bf16[256,768]{1,0:T(8,128)(2,1)S(1)}, bf16[256,768]{1,0:T(8,128)(2,1)S(1)}, u32[]{:S(2)}, u32[]{:S(2)}) collective-permute-start(bf16[256,768]{1,0:T(8,128)(2,1)S(1)} %get-tuple-element.76), channel_id=1, source_target_pairs={{16,0},{17,1},{18,2},{19,3},{20,4},{21,5},{22,6},{23,7},{24,8},{25... | collective-permute-start | bytes 1179656 | tf_op jit(solution)/shard_map/ppermute | solution.py:33
  379.7 62.4 %reduce-scatter.17.cloned.1.call-start = ((), (), s32[]{:S(2)}) async-start(), calls=%async_computation.13 | async-start | bytes 2211840 | tf_op jit(solution)/shard_map/reduce_scatter | solution.py:269
  385.3 96.5 %reduce-scatter.15.cloned.1.call-start = ((), (), s32[]{:S(2)}) async-start(), calls=%async_computation.12 | async-start | bytes 4423680 | tf_op jit(solution)/shard_map/reduce_scatter | solution.py:269
  393.8 131.2 %reduce-scatter.11.cloned.1.call-start = ((), (), s32[]{:S(2)}) async-start(), calls=%async_computation.10 | async-start | bytes 4423680 | tf_op jit(solution)/shard_map/reduce_scatter | solution.py:269
  407.9 10.0 %collective-permute-start.15 = (bf16[64,1536]{0,1:T(8,128)(2,1)S(1)}, bf16[64,1536]{0,1:T(8,128)(2,1)S(1)}, u32[]{:S(2)}, u32[]{:S(2)}) collective-permute-start(bf16[64,1536]{0,1:T(8,128)(2,1)S(1)} %get-tuple-element.85), channel_id=1, source_target_pairs={{4,0},{8,4},{12,8},{5,1},{9,5},{13,9},{6,2},{10,6},{14,10},{7,3},{... | collective-permute-start | bytes 589832 | tf_op jit(solution)/shard_map/ppermute | solution.py:23
  409.2 10.2 %collective-permute-start.14 = (bf16[64,1536]{0,1:T(8,128)(2,1)S(1)}, bf16[64,1536]{0,1:T(8,128)(2,1)S(1)}, u32[]{:S(2)}, u32[]{:S(2)}) collective-permute-start(bf16[64,1536]{0,1:T(8,128)(2,1)S(1)} %get-tuple-element.84), channel_id=1, source_target_pairs={{0,4},{4,8},{8,12},{1,5},{5,9},{9,13},{2,6},{6,10},{10,14},{3,7},{... | collective-permute-start | bytes 589832 | tf_op jit(solution)/shard_map/ppermute | solution.py:21
  439.3 107.9 %reduce-scatter.21.cloned.1.call-start = ((), (), s32[]{:S(2)}) async-start(), calls=%async_computation.15 | async-start | bytes 245760
  440.8 129.0 %reduce-scatter.19.cloned.1.call-start = ((), (), s32[]{:S(2)}) async-start(), calls=%async_computation.14 | async-start | bytes 245760
  441.8 232.4 %all-reduce.16.cloned.1.call-start = ((), (), s32[]{:S(2)}) async-start(), calls=%async_computation.16 | async-start | bytes 5013504 | tf_op jit(solution)/shard_map/psum | solution.py:271
  (150 other events, 574.8 us)
Sparse Core Ops, SparseCore 0:
  9.6 33.4 all-gather.4
  44.7 17.4 all-gather.6
  63.7 30.7 all-gather.8
  95.9 20.7 all-gather.10
  379.8 26.4 reduce-scatter.12
  409.4 29.3 reduce-scatter.16
  441.4 40.3 reduce-scatter.14
  484.5 40.4 reduce-scatter.10
  527.5 19.7 reduce-scatter.20
  550.1 19.7 reduce-scatter.18
  572.5 101.5 all-reduce.15
where the time goes:
time: 697 us; the launch traced here: 687 us
  waiting for transfers between devices  321 us (46%)
  matrix products  132 us (19%)
  local copies, waits for them, and re-layouts  76.1 us (11%)
  other arithmetic  70 us (10%)
  starting transfers between devices  50.6 us (7%)
  blocking collectives  20.2 us (3%)
  between operations  16.9 us (2%)
    psum x1, waiting for transfers between devices, body(): lax.psum(as_sent(owned), 'seq')  90.4 us
    reduce_scatter x4, waiting for transfers between devices, body(): lax.psum_scatter(as_sent(leading), 'fsdp', scatter_dimension=1, tiled=True)  82.9 us
    unnamed x13, waiting for transfers between devices  34.7 us
    unnamed x315, local copies, waits for them, and re-layouts  34.1 us
    ppermute x4, waiting for transfers between devices, from_behind(): return lax.ppermute(x, axis, pairs)  30.9 us
    ppermute x6, starting transfers between devices, padded(): lax.ppermute(tail, axis, [(i, (i + 1) % count) for i in range(ends)])  30 us
    sub x6, matrix products, attention_probs(): expo = jnp.exp(scores - top_score)  28.4 us
    all_gather x1, waiting for transfers between devices, body(): lax.all_gather(w_in, 'fsdp', axis=1, tiled=True)  26.6 us
  transfers between devices with their start and end apart: 27, of which 20 were waited for; matrix products, arithmetic and copies ran while one was open for 16% of the time, Pallas kernels for 0%

commit v1 on v0

v1 whole, which is shorter than its diff:
```python
import functools

import jax
import jax.numpy as jnp
from jax import lax
from jax.experimental import pallas as pl
from jax.experimental.pallas import tpu as pltpu
from jax.sharding import PartitionSpec as P

D = 768
HEAD_DIM = 64
FF = 1152
HALF = 64
PAIRS = D // 128
EPS = 1e-05
SCALE = HEAD_DIM ** (-0.5)
BF = jnp.bfloat16
F32 = jnp.float32
VMEM_LIMIT = 56 * 1024 * 1024
ANY = pl.BlockSpec(memory_space=pl.ANY)
VM = pl.BlockSpec(memory_space=pltpu.VMEM)


def dot_nn(x, y):
    return lax.dot_general(x, y, (((1,), (0,)), ((), ())), preferred_element_type=F32)


def dot_nt(x, y):
    return lax.dot_general(x, y, (((1,), (1,)), ((), ())), preferred_element_type=F32)


def dot_tn(x, y):
    return lax.dot_general(x, y, (((0,), (0,)), ((), ())), preferred_element_type=F32)


def normed_rows(v):
    centre = v - jnp.mean(v, axis=-1, keepdims=True)
    inv = lax.rsqrt(jnp.mean(centre * centre, axis=-1, keepdims=True) + EPS)
    return centre * inv, inv


def norm_back(grad, n, inv, gain):
    e = grad * gain
    return inv * (e - jnp.mean(e, axis=-1, keepdims=True) - n * jnp.mean(e * n, axis=-1, keepdims=True))


def two_heads(x):
    lane = lax.broadcasted_iota(jnp.int32, x.shape, 1)
    zero = jnp.zeros_like(x)
    return jnp.concatenate([jnp.where(lane < 64, x, zero), jnp.where(lane < 64, zero, x)], axis=0)


def one_of_two(x):
    rows = x.shape[0] // 2
    lane = lax.broadcasted_iota(jnp.int32, (rows, 128), 1)
    return jnp.where(lane < 64, x[:rows], x[rows:])


def allowed_mask(qb, start, seq_idx, seq_count, block_rows):
    shape = (2 * qb, qb + 2 * HALF)
    row = lax.broadcasted_iota(jnp.int32, shape, 0)
    row = jnp.where(row >= qb, row - qb, row)
    col = lax.broadcasted_iota(jnp.int32, shape, 1)
    rel = col - row
    key = seq_idx * block_rows + start - HALF + col
    return (rel >= 0) & (rel <= 2 * HALF) & (key >= 0) & (key < seq_count * block_rows)


def probs_of(q2, k, mask):
    scores = jnp.where(mask, dot_nt(q2, k) * SCALE, -1e30)
    expo = jnp.exp(scores - jnp.max(scores, axis=-1, keepdims=True))
    return expo / jnp.sum(expo, axis=-1, keepdims=True)


def forward_kernel(has_own, has_recv, seq_count, *refs):
    refs = list(refs)
    own = refs.pop(0) if has_own else None
    recv = [refs.pop(0) for _ in range(3)] if has_recv else None
    (gain_a, gain_f, w_qkv, w_out, w_in, w_ff, u_out, qkv_ref, o_ref, h_ref, gu_ref, out_ref,
     s_qkv, s_out, s_in, s_ff, sems) = refs
    copies = [pltpu.make_async_copy(src, dst, sems.at[i]) for i, (src, dst) in
              enumerate(((w_qkv, s_qkv), (w_out, s_out), (w_in, s_in), (w_ff, s_ff)))]
    for copy in copies:
        copy.start()
    rows = out_ref.shape[0]
    sec = lax.axis_index("section")
    seq_idx = lax.axis_index("seq")
    if has_recv:
        u_b = jnp.concatenate([recv[1][...], recv[0][...], recv[2][...]], axis=0)
        if has_own:
            pick = (jnp.zeros(u_b.shape, jnp.int32) + sec) == 0
            u_f = jnp.where(pick, own[...].astype(F32), u_b.astype(F32))
            u_b = u_f.astype(BF)
    else:
        u_b = own[...]
    u_out[...] = u_b
    u = u_b.astype(F32)
    a = (normed_rows(u)[0] * gain_a[...]).astype(BF)
    copies[0].wait()
    qkv_ref[...] = dot_nn(a, s_qkv[...]).astype(BF)
    qb = min(rows, 128)
    for start in range(0, rows, qb):
        mask = allowed_mask(qb, start, seq_idx, seq_count, rows)
        span = slice(start, start + qb + 2 * HALF)
        for p in range(PAIRS):
            lanes = slice(p * 128, p * 128 + 128)
            q2 = two_heads(qkv_ref[HALF + start:HALF + start + qb, lanes])
            k = qkv_ref[span, D + p * 128:D + p * 128 + 128]
            v = qkv_ref[span, 2 * D + p * 128:2 * D + p * 128 + 128]
            mixed = dot_nn(probs_of(q2, k, mask).astype(BF), v)
            o_ref[start:start + qb, lanes] = one_of_two(mixed).astype(BF)
    copies[1].wait()
    h = u_out[HALF:HALF + rows].astype(F32) + dot_nn(o_ref[...], s_out[...])
    h_ref[...] = h
    b = (normed_rows(h)[0] * gain_f[...]).astype(BF)
    copies[2].wait()
    gu_ref[...] = dot_nn(b, s_in[...])
    gate = gu_ref[:, :FF]
    hid = (0.5 * gate * (1.0 + lax.erf(gate * 0.7071067811865476)) * gu_ref[:, FF:]).astype(BF)
    copies[3].wait()
    out_ref[...] = (h_ref[...] + dot_nn(hid, s_ff[...])).astype(BF)


WEIGHT_SCRATCH = [
    pltpu.VMEM((D, 3 * D), BF),
    pltpu.VMEM((D, D), BF),
    pltpu.VMEM((D, 2 * FF), BF),
    pltpu.VMEM((FF, D), BF),
]


def forward_call(own, recv, gains, mats, rows, seq_count):
    ext = rows + 2 * HALF
    args = ([own] if own is not None else []) + (list(recv) if recv is not None else [])
    shape = jax.ShapeDtypeStruct
    return pl.pallas_call(
        functools.partial(forward_kernel, own is not None, recv is not None, seq_count),
        out_shape=(shape((ext, D), BF), shape((ext, 3 * D), BF), shape((rows, D), BF),
                   shape((rows, D), F32), shape((rows, 2 * FF), F32), shape((rows, D), BF)),
        in_specs=[VM] * (len(args) + 2) + [ANY] * 4,
        out_specs=(VM,) * 6,
        scratch_shapes=WEIGHT_SCRATCH + [pltpu.SemaphoreType.DMA((4,))],
        compiler_params=pltpu.CompilerParams(vmem_limit_bytes=VMEM_LIMIT),
    )(*args, *gains, *mats)


def backward_kernel(has_cot, has_recv, same, seq_count, *refs):
    refs = list(refs)
    cot = refs.pop(0) if has_cot else None
    recv = [refs.pop(0) for _ in range(3)] if has_recv else None
    gain_a, gain_f = refs[:2]
    weights = refs[2:6]
    refs = refs[6:]
    kept_a, refs = refs[:5], refs[5:]
    kept_b, refs = refs[:5], refs[5:]
    (du_ref, du_b_ref, rim_ref, a_ref, dqkv_ref, o_out, dattn_ref, b_ref, dgu_ref, hid_ref, dff_ref,
     ga_ref, gf_ref) = refs[:13]
    s_qkv, s_out, s_in, s_ff, u_s, qkv_s, h_s, gu_s, dout, do_s, acc, sems = refs[13:]
    kept_s = (u_s, qkv_s, o_out, h_s, gu_s)
    rows = du_ref.shape[0]
    ext = rows + 2 * HALF
    sec = lax.axis_index("section")
    seq_idx = lax.axis_index("seq")

    @pl.when(sec == 0)
    def _():
        for i in (4, 3, 0, 1, 2):
            pltpu.make_async_copy(kept_a[i], kept_s[i], sems.at[4 + i]).start()

    @pl.when(sec != 0)
    def _():
        for i in (4, 3, 0, 1, 2):
            pltpu.make_async_copy(kept_b[i], kept_s[i], sems.at[4 + i]).start()

    kept_copies = [pltpu.make_async_copy(kept_a[i], kept_s[i], sems.at[4 + i]) for i in range(5)]
    copies = [pltpu.make_async_copy(src, dst, sems.at[i]) for i, (src, dst) in
              enumerate(zip(weights, (s_qkv, s_out, s_in, s_ff)))]
    for i in (3, 2, 1, 0):
        copies[i].start()
    if has_recv:
        dout[...] = recv[0][...].astype(F32)
        dout[0:HALF] += recv[1][...].astype(F32)
        dout[rows - HALF:rows] += recv[2][...].astype(F32)
        got = dout[...].astype(BF).astype(F32)
    else:
        got = jnp.zeros((rows, D), F32)
    if has_cot:
        pick = (jnp.zeros((rows, D), jnp.int32) + sec) == 1
        got = jnp.where(pick, cot[...].astype(F32), got)
    dout[...] = got
    dff_ref[...] = got.astype(BF)
    copies[3].wait()
    dhid = dot_nt(dff_ref[...], s_ff[...])
    kept_copies[4].wait()
    gate, up = gu_s[:, :FF], gu_s[:, FF:]
    cdf = 0.5 * (1.0 + lax.erf(gate * 0.7071067811865476))
    act = gate * cdf
    hid_ref[...] = (act * up).astype(BF)
    pdf = jnp.exp(-0.5 * gate * gate) * 0.3989422804014327
    dgu_ref[:, :FF] = (dhid * up * (cdf + gate * pdf)).astype(BF)
    dgu_ref[:, FF:] = (dhid * act).astype(BF)
    copies[2].wait()
    db = dot_nt(dgu_ref[...], s_in[...])
    kept_copies[3].wait()
    n, inv = normed_rows(h_s[...])
    b_ref[...] = (n * gain_f[...]).astype(BF)
    gf_ref[...] = jnp.sum(db * n, axis=0, keepdims=True)
    dout[...] += norm_back(db, n, inv, gain_f[...])
    dattn_ref[...] = dout[...].astype(BF)
    copies[1].wait()
    do_s[...] = dot_nt(dattn_ref[...], s_out[...]).astype(BF)
    kept_copies[0].wait()
    kept_copies[1].wait()
    kept_copies[2].wait()
    acc[...] = jnp.zeros_like(acc)
    dqkv_ref[0:HALF, 0:D] = jnp.zeros((HALF, D), BF)
    dqkv_ref[ext - HALF:ext, 0:D] = jnp.zeros((HALF, D), BF)
    qb = min(rows, 128)
    for start in range(0, rows, qb):
        mask = allowed_mask(qb, start, seq_idx, seq_count, rows)
        span = slice(start, start + qb + 2 * HALF)
        mid = slice(HALF + start, HALF + start + qb)
        for p in range(PAIRS):
            lanes = slice(p * 128, p * 128 + 128)
            klanes = slice(D + p * 128, D + p * 128 + 128)
            vlanes = slice(2 * D + p * 128, 2 * D + p * 128 + 128)
            q2 = two_heads(qkv_s[mid, lanes])
            k = qkv_s[span, klanes]
            v = qkv_s[span, vlanes]
            do2 = two_heads(do_s[start:start + qb, lanes])
            probs = probs_of(q2, k, mask)
            dp = dot_nt(do2, v)
            ds = (probs * (dp - jnp.sum(probs * dp, axis=-1, keepdims=True))).astype(BF)
            dqkv_ref[mid, lanes] = (one_of_two(dot_nn(ds, k)) * SCALE).astype(BF)
            acc[span, lanes] += dot_tn(ds, q2) * SCALE
            acc[span, klanes] += dot_tn(probs.astype(BF), do2)
    dqkv_ref[:, D:] = acc[...].astype(BF)
    copies[0].wait()
    da = dot_nt(dqkv_ref[...], s_qkv[...])
    m, inv_u = normed_rows(u_s[...].astype(F32))
    a_ref[...] = (m * gain_a[...]).astype(BF)
    ga_ref[...] = jnp.sum(da * m, axis=0, keepdims=True)
    du = norm_back(da, m, inv_u, gain_a[...])
    rim_ref[0:HALF] = du[:HALF].astype(BF)
    rim_ref[HALF:2 * HALF] = du[ext - HALF:].astype(BF)
    du_mid = dout[...] + du[HALF:HALF + rows]
    du_ref[...] = du_mid
    du_b_ref[...] = du_mid.astype(BF)


def backward_call(cot, recv, gains, mats, kept_a, kept_b, rows, seq_count):
    ext = rows + 2 * HALF
    args = ([cot] if cot is not None else []) + (list(recv) if recv is not None else [])
    shape = jax.ShapeDtypeStruct
    return pl.pallas_call(
        functools.partial(backward_kernel, cot is not None, recv is not None, False, seq_count),
        out_shape=(shape((rows, D), F32), shape((rows, D), BF), shape((2 * HALF, D), BF), shape((ext, D), BF),
                   shape((ext, 3 * D), BF), shape((rows, D), BF), shape((rows, D), BF),
                   shape((rows, D), BF), shape((rows, 2 * FF), BF), shape((rows, FF), BF),
                   shape((rows, D), BF), shape((1, D), F32), shape((1, D), F32)),
        in_specs=[VM] * (len(args) + 2) + [ANY] * 14,
        out_specs=(VM,) * 13,
        scratch_shapes=WEIGHT_SCRATCH + [
            pltpu.VMEM((ext, D), BF), pltpu.VMEM((ext, 3 * D), BF), pltpu.VMEM((rows, D), F32),
            pltpu.VMEM((rows, 2 * FF), F32), pltpu.VMEM((rows, D), F32), pltpu.VMEM((rows, D), BF),
            pltpu.VMEM((ext, 2 * D), F32), pltpu.SemaphoreType.DMA((9,)),
        ],
        compiler_params=pltpu.CompilerParams(vmem_limit_bytes=VMEM_LIMIT),
    )(*args, *gains, *mats, *kept_a, *kept_b)


def weight_kernel(*refs):
    slots = (refs[0:8], refs[8:16], refs[16:24])
    outs = refs[24:28]
    bufs = refs[28:36]
    sems = refs[36]
    sec = lax.axis_index("section")
    order = (6, 7, 4, 5, 2, 3, 0, 1)

    def copy(slot, i, part):
        rows = slots[slot][i].shape[0]
        return pltpu.make_async_copy(slots[slot][i], bufs[i].at[pl.ds(part * rows, rows)],
                                     sems.at[part, i])

    for i in order:
        copy(1, i, 0).start()

        @pl.when(sec == 0)
        def _():
            copy(2, i, 1).start()

        @pl.when(sec != 0)
        def _():
            copy(0, i, 1).start()

    for w in (3, 2, 1, 0):
        for i in (2 * w, 2 * w + 1):
            copy(1, i, 0).wait()
            copy(2, i, 1).wait()
        left = bufs[2 * w][...]
        width = outs[w].shape[1]
        step = 384
        for c in range(0, width, step):
            outs[w][:, c:c + step] = dot_tn(left, bufs[2 * w + 1][:, c:c + step]).astype(BF)


def weight_call(slots):
    shape = jax.ShapeDtypeStruct
    scratch = [pltpu.VMEM((2 * x.shape[0], x.shape[1]), BF) for x in slots[0]]
    return pl.pallas_call(
        weight_kernel,
        out_shape=(shape((D, 3 * D), BF), shape((D, D), BF), shape((D, 2 * FF), BF), shape((FF, D), BF)),
        in_specs=[ANY] * 24,
        out_specs=(VM,) * 4,
        scratch_shapes=scratch + [pltpu.SemaphoreType.DMA((2, 8))],
        compiler_params=pltpu.CompilerParams(vmem_limit_bytes=VMEM_LIMIT),
    )(*slots[0], *slots[1], *slots[2])


def neighbours(seq_count, from_sec, to_sec, by):
    return [(from_sec * seq_count + i, to_sec * seq_count + i + by)
            for i in range(seq_count) if 0 <= i + by < seq_count]


def body(inputs, cotangent, w_qkv, w_attn_out, w_in, w_ff_out, ln_attn, ln_ff):
    sec = lax.axis_index("section")
    seq_count = lax.axis_size("seq")
    rows = inputs.shape[2]
    axes = ("section", "seq")
    x = inputs[:, 0]
    right = [(i, i + 1) for i in range(seq_count - 1)]
    left = [(i + 1, i) for i in range(seq_count - 1)]
    from_left = lax.ppermute(x[:, rows - HALF:], "seq", right)
    from_right = lax.ppermute(x[:, :HALF], "seq", left)
    own = jnp.concatenate([from_left, x, from_right], axis=1)
    mats = tuple(lax.all_gather(w[0], "fsdp", axis=0, tiled=True) for w in (w_qkv, w_attn_out, w_in, w_ff_out))
    gains = lax.all_gather(jnp.concatenate([ln_attn, ln_ff], axis=0), "fsdp", axis=1, tiled=True).astype(F32)
    gains = (gains[0:1], gains[1:2])

    def relay(out):
        return (
            lax.ppermute(out, "section", [(0, 1)]),
            lax.ppermute(out[rows - HALF:], axes, neighbours(seq_count, 0, 1, 1)),
            lax.ppermute(out[:HALF], axes, neighbours(seq_count, 0, 1, -1)),
        )

    def relay_back(du_b, rim):
        return (
            lax.ppermute(du_b, "section", [(1, 0)]),
            lax.ppermute(rim[HALF:], axes, neighbours(seq_count, 1, 0, 1)),
            lax.ppermute(rim[:HALF], axes, neighbours(seq_count, 1, 0, -1)),
        )

    kept0 = forward_call(own[0], None, gains, mats, rows, seq_count)
    kept1 = forward_call(own[1], relay(kept0[5]), gains, mats, rows, seq_count)
    kept2 = forward_call(None, relay(kept1[5]), gains, mats, rows, seq_count)
    kept = [k[:5] for k in (kept0, kept1, kept2)]
    cot = cotangent[:, 0]
    back0 = backward_call(cot[0], None, gains, mats, kept[0], kept[1], rows, seq_count)
    back1 = backward_call(cot[1], relay_back(back0[1], back0[2]), gains, mats, kept[0], kept[2], rows, seq_count)
    back2 = backward_call(None, relay_back(back1[1], back1[2]), gains, mats, kept[1], kept[2], rows, seq_count)
    backs = (back0, back1, back2)
    rims = jnp.where(sec == 0, jnp.stack([back1[2], back2[2]]), jnp.stack([back0[2], back1[2]]))
    to_right = lax.ppermute(rims[:, HALF:], "seq", right).astype(F32)
    to_left = lax.ppermute(rims[:, :HALF], "seq", left).astype(F32)
    totals = weight_call([b[3:11] for b in backs])
    ln_totals = jnp.concatenate([sum(b[11] for b in backs), sum(b[12] for b in backs)], axis=0)
    owned = tuple(lax.psum_scatter(t, "fsdp", scatter_dimension=0, tiled=True) for t in totals)
    owned_ln = lax.psum_scatter(ln_totals.astype(BF), "fsdp", scatter_dimension=1, tiled=True)
    summed = lax.psum(owned + (owned_ln,), "seq")
    summed = tuple(s.astype(F32) for s in summed)
    layer_out = jnp.where(sec == 0, jnp.stack([kept0[5], kept1[5]]), jnp.stack([kept1[5], kept2[5]]))
    grad = jnp.where(sec == 0, jnp.stack([back1[0], back2[0]]), jnp.stack([back0[0], back1[0]]))
    pad = ((0, 0), (0, rows - HALF), (0, 0))
    grad = grad + jnp.pad(to_right, pad)
    grad = grad + jnp.pad(to_left, (pad[0], pad[1][::-1], pad[2]))
    grad = jnp.where(sec == 1, grad.astype(BF).astype(F32), grad)
    return (layer_out[None, :, None], grad[None, :, None], summed[0][None], summed[1][None], summed[2][None],
            summed[3][None], summed[4][0:1], summed[4][1:2])


def solution(mesh):
    placed = (
        P(None, "fsdp", "seq", None),
        P(None, "fsdp", "seq", None),
        P("section", "fsdp", None),
        P("section", "fsdp", None),
        P("section", "fsdp", None),
        P("section", "fsdp", None),
        P("section", "fsdp"),
        P("section", "fsdp"),
    )
    return jax.shard_map(
        body,
        mesh=mesh,
        in_specs=placed,
        out_specs=(
            P("section", None, "fsdp", "seq", None),
            P("section", None, "fsdp", "seq", None),
            P("section", "fsdp", None),
            P("section", "fsdp", None),
            P("section", "fsdp", None),
            P("section", "fsdp", None),
            P("section", "fsdp"),
            P("section", "fsdp"),
        ),
        check_vma=False,
    )
```

time: 697 us -> 564 us (0.81)
  matrix products: 132 us -> 0 us
  Pallas kernels: 0 us -> 105 us
  local copies, waits for them, and re-layouts: 76.1 us -> 11.8 us
  other arithmetic: 70 us -> 11.3 us
  waiting for transfers between devices: 321 us -> 360 us
  starting transfers between devices: 50.6 us -> 38.8 us
    pallas_call x0 -> x7, Pallas kernels: none -> 105 us  [the longest x3 57.4 us: backward_call(): pl.pallas_call(functools.partial(backward_kernel, cot is not None, recv i...]
    dot_general x43 -> x0, matrix products: 104 us -> none  [the longest x3 13.6 us: body(): jnp.dot(forward_hidden, mat_ff, preferred_element_type=jnp.float32)]
    reduce_scatter x4, waiting for transfers between devices: 82.9 us -> 141 us  [body(): lax.psum_scatter(t, 'fsdp', scatter_dimension=0, tiled=True)]
    unnamed x315 -> x64, local copies, waits for them, and re-layouts: 34.1 us -> 5.49 us
    sub x6 -> x0, matrix products: 28.4 us -> none  [attention_probs(): expo = jnp.exp(scores - top_score)]
    convert_element_type x27 -> x1, other arithmetic: 27.5 us -> 0.01 us  [body(): lax.all_gather(jnp.concatenate([ln_attn, ln_ff], axis=0), 'fsdp', axis=1,...]
    ppermute x16, waiting for transfers between devices: 45.1 us -> 17.8 us  [the longest x2 6.22 us: relay_back(): lax.ppermute(rim[:HALF], axes, neighbours(seq_count, 1, 0, -1))]
    all_gather x4, waiting for transfers between devices: 67.4 us -> 92.3 us  [body(): lax.all_gather(w[0], 'fsdp', axis=0, tiled=True)]
  transfers between devices with their start and end apart: 27 -> 26, of which waited for: 20 -> 15; matrix products, arithmetic and copies ran while one was open for 16% -> 2% of each run, Pallas kernels for 0% -> 5%
where the time goes in v1:
time: 564 us; the launch traced here: 558 us
  waiting for transfers between devices  360 us (64%)
  Pallas kernels  105 us (19%)
  starting transfers between devices  38.8 us (7%)
  blocking collectives  17 us (3%)
  between operations  15 us (3%)
  local copies, waits for them, and re-layouts  11.8 us (2%)
  other arithmetic  11.3 us (2%)
    reduce_scatter x4, waiting for transfers between devices, body(): lax.psum_scatter(t, 'fsdp', scatter_dimension=0, tiled=True)  141 us
    all_gather x4, waiting for transfers between devices, body(): lax.all_gather(w[0], 'fsdp', axis=0, tiled=True)  92.3 us
    psum x1, waiting for transfers between devices, body(): summed = lax.psum(owned + (owned_ln,), 'seq')  89.4 us
    pallas_call x3, Pallas kernels, backward_call(): pl.pallas_call(functools.partial(backward_kernel, cot is not None, recv i...  57.4 us
    pallas_call x3, Pallas kernels, forward_call(): pl.pallas_call(functools.partial(forward_kernel, own is not None, recv is...  34.7 us
    unnamed x11, waiting for transfers between devices  19.3 us
    pallas_call x1, Pallas kernels, weight_call(): pl.pallas_call(weight_kernel, out_shape=(shape((D, 3 * D), BF), shape((D,...  12.5 us
    psum x1, blocking collectives, body(): summed = lax.psum(owned + (owned_ln,), 'seq')  11.9 us
  transfers between devices with their start and end apart: 26, of which 15 were waited for; matrix products, arithmetic and copies ran while one was open for 2% of the time, Pallas kernels for 5%

profile of v1, /device:TPU:0, one launch (start us, length us, event | category | flops | bytes accessed | tf_op | source)
XLA Modules:
  0.0 558.0 jit_solution(16257818559310983267)
XLA Ops:
  10.1 4.9 collective-permute-start
  16.4 5.1 all-gather.4
  24.5 5.3 all-gather.12.cloned.1.call-done
  29.8 22.4 %all-gather.16.cloned.1.call-done = bf16[1,1152,768]{2,1,0:T(8,128)(2,1)} async-done(((bf16[1,288,768]{2,1,0:T(8,128)(2,1)}), bf16[1,1152,768]{2,1,0:T(8,128)(2,1)}) %all-gather.16.cloned.1.call-update) | async-done | bytes 1769488 | tf_op jit(solution)/shard_map/all_gather | solution.py:336
  52.1 32.4 %all-gather.10.cloned.1.call-done = bf16[1,768,2304]{2,1,0:T(8,128)(2,1)} async-done(((bf16[1,192,2304]{2,1,0:T(8,128)(2,1)}), bf16[1,768,2304]{2,1,0:T(8,128)(2,1)}) %all-gather.10.cloned.1.call-update) | async-done | bytes 3538960 | tf_op jit(solution)/shard_map/all_gather | solution.py:336
  84.5 32.2 %all-gather.14.cloned.1.call-done = bf16[1,768,2304]{2,1,0:T(8,128)(2,1)} async-done(((bf16[1,192,2304]{2,1,0:T(8,128)(2,1)}), bf16[1,768,2304]{2,1,0:T(8,128)(2,1)}) %all-gather.14.cloned.1.call-update) | async-done | bytes 3538960 | tf_op jit(solution)/shard_map/all_gather | solution.py:336
  116.7 11.6 %shard_map.143 = (bf16[384,768]{1,0:T(8,128)(2,1)}, bf16[384,2304]{1,0:T(8,128)(2,1)}, bf16[256,768]{1,0:T(8,128)(2,1)}, f32[256,768]{1,0:T(8,128)}, f32[256,2304]{1,0:T(8,128)}, /*index=5*/bf16[256,768]{1,0:T(8,128)(2,1)}) custom-call(bf16[384,768]{1,0:T(8,128)(2,1)} %get-tuple-element.156.refs_0_, f32[1,768]{1,0:T(1,128)} %get-tuple-element.173.refs_1_.refs_4_.refs_3_, ...), custom_call_target="tpu_custom_call" | custom-call | tf_op jit(solution)/shard_map/pallas_call | solution.py:136
  128.3 3.4 collective-permute-start.2
  133.3 3.0 collective-permute-start.3
  137.3 2.2 collective-permute-done.3.refs_2_
  139.5 3.4 collective-permute-done.2.refs_1_
  143.6 11.7 %shard_map.144 = (bf16[384,768]{1,0:T(8,128)(2,1)}, bf16[384,2304]{1,0:T(8,128)(2,1)}, bf16[256,768]{1,0:T(8,128)(2,1)}, f32[256,768]{1,0:T(8,128)}, f32[256,2304]{1,0:T(8,128)}, /*index=5*/bf16[256,768]{1,0:T(8,128)(2,1)}) custom-call(bf16[384,768]{1,0:T(8,128)(2,1)} %get-tuple-element.157.refs_0_, bf16[256,768]{1,0:T(8,128)(2,1)} %copy-done.12, ...), custom_call_target="tpu_custom_call" | custom-call | tf_op jit(solution)/shard_map/pallas_call | solution.py:136
  155.3 4.5 collective-permute-start.5
  159.8 19.0 %shard_map.146 = (f32[256,768]{1,0:T(8,128)}, bf16[256,768]{1,0:T(8,128)(2,1)}, bf16[128,768]{1,0:T(8,128)(2,1)}, bf16[384,768]{1,0:T(8,128)(2,1)}, bf16[384,230...) custom-call(bf16[256,768]{1,0:T(8,128)(2,1)} %get-tuple-element.158., ...), custom_call_target="tpu_custom_call" | custom-call | tf_op jit(solution)/shard_map/pallas_call | solution.py:255
  180.8 8.2 %collective-permute-start.6 = (bf16[64,768]{1,0:T(8,128)(2,1)S(1)}, bf16[64,768]{1,0:T(8,128)(2,1)S(1)}, u32[]{:S(2)}, u32[]{:S(2)}) collective-permute-start(bf16[64,768]{1,0:T(8,128)(2,1)S(1)} %get-tuple-element.165), channel_id=1, source_target_pairs={{0,20},{4,24},{8,28},{1,21},{5,25},{9,29},{2,22},{6,26},{10,30},{3... | collective-permute-start | bytes 294920 | tf_op jit(solution)/shard_map/ppermute | solution.py:343
  193.9 11.5 %shard_map.145 = (bf16[384,768]{1,0:T(8,128)(2,1)}, bf16[384,2304]{1,0:T(8,128)(2,1)}, bf16[256,768]{1,0:T(8,128)(2,1)}, f32[256,768]{1,0:T(8,128)}, f32[256,2304]{1,0:T(8,128)}, /*index=5*/bf16[256,768]{1,0:T(8,128)(2,1)}) custom-call(bf16[256,768]{1,0:T(8,128)(2,1)} %copy-done.11, bf16[64,768]{1,0:T(8,128)(2,1)} %copy-done.20, bf16[64,768]{1,0:T(8,128)(2,1)} %copy-done.19, ...), custom_call_target="tpu_custom_call" | custom-call | tf_op jit(solution)/shard_map/pallas_call | solution.py:136
  206.2 19.4 %shard_map.147 = (f32[256,768]{1,0:T(8,128)}, bf16[256,768]{1,0:T(8,128)(2,1)}, bf16[128,768]{1,0:T(8,128)(2,1)}, bf16[384,768]{1,0:T(8,128)(2,1)}, bf16[384,230...) custom-call(bf16[256,768]{1,0:T(8,128)(2,1)} %get-tuple-element.159., ...), custom_call_target="tpu_custom_call" | custom-call | tf_op jit(solution)/shard_map/pallas_call | solution.py:255
  229.9 6.2 %collective-permute-done.13.refs_2_ = bf16[64,768]{1,0:T(8,128)(2,1)S(1)} collective-permute-done((bf16[64,768]{1,0:T(8,128)(2,1)S(1)}, bf16[64,768]{1,0:T(8,128)(2,1)S(1)}, u32[]{:S(2)}, u32[]{:S(2)}) %collective-permute-start.13) | collective-permute-done | bytes 98336 | tf_op jit(solution)/shard_map/ppermute | solution.py:351
  236.1 4.9 collective-permute-done.11.refs_0_
  241.8 19.0 %shard_map.148 = (f32[256,768]{1,0:T(8,128)}, bf16[256,768]{1,0:T(8,128)(2,1)}, bf16[128,768]{1,0:T(8,128)(2,1)}, bf16[384,768]{1,0:T(8,128)(2,1)}, bf16[384,230...) custom-call(bf16[256,768]{1,0:T(8,128)(2,1)} %copy-done.14, ...), custom_call_target="tpu_custom_call" | custom-call | tf_op jit(solution)/shard_map/pallas_call | solution.py:255
  260.8 12.5 %shard_map.149 = (bf16[768,2304]{1,0:T(8,128)(2,1)}, bf16[768,768]{1,0:T(8,128)(2,1)}, bf16[768,2304]{1,0:T(8,128)(2,1)}, bf16[1152,768]{1,0:T(8,128)(2,1)}) custom-call(bf16[384,768]{1,0:T(8,128)(2,1)} %get-tuple-element.94.refs_0_, bf16[384,2304]{1,0:T(8,128)(2,1)} %get-tuple-element.95.refs_1_, bf16[256,768]{1,0:T(8,128)(2,1)} %get-tuple-element.96.refs_2_, ...), custom_call_target="tpu_custom_call" | custom-call | tf_op jit(solution)/shard_map/pallas_call | solution.py:310
  276.5 22.1 %reduce-scatter.10.cloned.1.call-done = bf16[192,768]{1,0:T(8,128)(2,1)} async-done(((bf16[768,768]{1,0:T(8,128)(2,1)}), bf16[192,768]{1,0:T(8,128)(2,1)}) %reduce-scatter.10.cloned.1.call-update) | async-done | bytes 294928 | tf_op jit(solution)/shard_map/reduce_scatter | solution.py:368
  298.5 32.6 %reduce-scatter.14.cloned.1.call-done = bf16[288,768]{1,0:T(8,128)(2,1)} async-done(((bf16[1152,768]{1,0:T(8,128)(2,1)}), bf16[288,768]{1,0:T(8,128)(2,1)}) %reduce-scatter.14.cloned.1.call-update) | async-done | bytes 442384 | tf_op jit(solution)/shard_map/reduce_scatter | solution.py:368
  331.1 43.0 %reduce-scatter.8.cloned.1.call-done = bf16[192,2304]{1,0:T(8,128)(2,1)} async-done(((bf16[768,2304]{1,0:T(8,128)(2,1)}), bf16[192,2304]{1,0:T(8,128)(2,1)}) %reduce-scatter.8.cloned.1.call-update) | async-done | bytes 884752 | tf_op jit(solution)/shard_map/reduce_scatter | solution.py:368
  374.1 43.2 %reduce-scatter.12.cloned.1.call-done = bf16[192,2304]{1,0:T(8,128)(2,1)} async-done(((bf16[768,2304]{1,0:T(8,128)(2,1)}), bf16[192,2304]{1,0:T(8,128)(2,1)}) %reduce-scatter.12.cloned.1.call-update) | async-done | bytes 884752 | tf_op jit(solution)/shard_map/reduce_scatter | solution.py:368
  417.4 2.1 maximum_select_fusion.1
  420.6 3.4 collective-permute-start.14
  425.3 14.8 %reduce-scatter.16.cloned.1.call-done = bf16[192,2]{1,0:T(8,128)(2,1)} async-done(((bf16[768,2]{1,0:T(8,128)(2,1)}), bf16[192,2]{1,0:T(8,128)(2,1)}) %reduce-scatter.16.cloned.1.call-update) | async-done | bytes 784
  441.0 11.9 %psum.39 = bf16[2,192]{1,0:T(2,128)(2,1)S(1)} all-reduce(bf16[2,192]{1,0:T(2,128)(2,1)S(1)} %copy.23), channel_id=1, replica_groups=mesh['section'=2,'seq'=4,'fsdp'=4] {'seq'}, use_global_device_ids=true, to_apply=%region_9.10 | all-reduce | flops 384 | bytes 1536 | tf_op jit(solution)/shard_map/psum | solution.py:370
  454.8 89.4 %all-reduce.5.cloned.1.call-done = (bf16[1,192,2304]{2,1,0:T(8,128)(2,1)}, bf16[1,192,768]{2,1,0:T(8,128)(2,1)}, bf16[1,192,2304]{2,1,0:T(8,128)(2,1)}, bf16[1,288,768]{2,1,0:T(8,128)(2,1)}) async-done(((bf16[1,192,2304]{2,1,0:T(8,128)(2,1)}, bf16[1,192,768]{2,1,0:T(8,128)(2,1)}, bf16[1,192,2304]{2,1,0:T(8,128)(2,1)}, bf16[1,288,768]{2,1,0:T(8,128)(2,1)}), (bf16[1,192,2304]{2,1,0:T(8,128)(2,1)}, ...) | async-done | bytes 2506768 | tf_op jit(solution)/shard_map/psum | solution.py:370
  544.2 1.9 broadcast_in_dim.32
  546.1 2.6 broadcast_in_dim.30
  (126 shorter events, 33.4 us)
Async XLA Ops:
  7.2 22.6 %all-gather.12.cloned.1.call-start = ((), (), s32[]{:S(2)}) async-start(), calls=%async_computation.10 | async-start | bytes 1474560 | tf_op jit(solution)/shard_map/all_gather | solution.py:336
  7.9 44.2 %all-gather.16.cloned.1.call-start = ((), (), s32[]{:S(2)}) async-start(), calls=%async_computation.12 | async-start | bytes 2211840 | tf_op jit(solution)/shard_map/all_gather | solution.py:336
  8.7 75.8 %all-gather.10.cloned.1.call-start = ((), (), s32[]{:S(2)}) async-start(), calls=%async_computation.9 | async-start | bytes 4423680 | tf_op jit(solution)/shard_map/all_gather | solution.py:336
  9.4 107.3 %all-gather.14.cloned.1.call-start = ((), (), s32[]{:S(2)}) async-start(), calls=%async_computation.11 | async-start | bytes 4423680 | tf_op jit(solution)/shard_map/all_gather | solution.py:336
  10.0 288.6 %reduce-scatter.10.cloned.1.call-start = ((), (), s32[]{:S(2)}) async-start(), calls=%async_computation.6 | async-start | bytes 1474560 | tf_op jit(solution)/shard_map/reduce_scatter | solution.py:368
  10.1 12.1 %collective-permute-start = (bf16[2,64,768]{2,1,0:T(8,128)(2,1)S(1)}, bf16[2,64,768]{2,1,0:T(8,128)(2,1)S(1)}, u32[]{:S(2)}, u32[]{:S(2)}) collective-permute-start(bf16[2,64,768]{2,1,0:T(8,128)(2,1)S(1)} %get-tuple-element.160), channel_id=1, source_target_pairs={{0,4},{4,8},{8,12},{1,5},{5,9},{9,13},{2,6},{6,10},{10,14},{3,7},{... | collective-permute-start | bytes 589832 | tf_op jit(solution)/shard_map/ppermute | solution.py:333
  15.0 8.3 %collective-permute-start.1 = (bf16[2,64,768]{2,1,0:T(8,128)(2,1)S(1)}, bf16[2,64,768]{2,1,0:T(8,128)(2,1)S(1)}, u32[]{:S(2)}, u32[]{:S(2)}) collective-permute-start(bf16[2,64,768]{2,1,0:T(8,128)(2,1)S(1)} %get-tuple-element.161), channel_id=1, source_target_pairs={{4,0},{8,4},{12,8},{5,1},{9,5},{13,9},{6,2},{10,6},{14,10},{7,3},{... | collective-permute-start | bytes 589832 | tf_op jit(solution)/shard_map/ppermute | solution.py:334
  116.7 19.6 %copy-start.9 = (bf16[2,1,256,768]{3,2,1,0:T(8,128)(2,1)S(1)}, bf16[2,1,256,768]{3,2,1,0:T(8,128)(2,1)}, u32[]{:S(2)}) copy-start(bf16[2,1,256,768]{3,2,1,0:T(8,128)(2,1)} %param.9) | copy-start | bytes 2359300
  128.3 14.6 %collective-permute-start.2 = (bf16[256,768]{1,0:T(8,128)(2,1)}, bf16[256,768]{1,0:T(8,128)(2,1)S(1)}, u32[]{:S(2)}, u32[]{:S(2)}) collective-permute-start(bf16[256,768]{1,0:T(8,128)(2,1)} %get-tuple-element.68), channel_id=1, source_target_pairs={{0,16},{1,17},{2,18},{3,19},{4,20},{5,21},{6,22},{7,23},{8,24},{9,... | collective-permute-start | bytes 1179656 | tf_op jit(solution)/shard_map/ppermute | solution.py:342
  132.7 4.7 collective-permute-start.4
  133.3 6.2 %collective-permute-start.3 = (bf16[64,768]{1,0:T(8,128)(2,1)S(1)}, bf16[64,768]{1,0:T(8,128)(2,1)S(1)}, u32[]{:S(2)}, u32[]{:S(2)}) collective-permute-start(bf16[64,768]{1,0:T(8,128)(2,1)S(1)} %get-tuple-element.167), channel_id=1, source_target_pairs={{0,20},{4,24},{8,28},{1,21},{5,25},{9,29},{2,22},{6,26},{10,30},{3... | collective-permute-start | bytes 294920 | tf_op jit(solution)/shard_map/ppermute | solution.py:343
  155.3 37.2 %collective-permute-start.5 = (bf16[256,768]{1,0:T(8,128)(2,1)}, bf16[256,768]{1,0:T(8,128)(2,1)S(1)}, u32[]{:S(2)}, u32[]{:S(2)}) collective-permute-start(bf16[256,768]{1,0:T(8,128)(2,1)} %get-tuple-element.69), channel_id=1, source_target_pairs={{0,16},{1,17},{2,18},{3,19},{4,20},{5,21},{6,22},{7,23},{8,24},{9,... | collective-permute-start | bytes 1179656 | tf_op jit(solution)/shard_map/ppermute | solution.py:342
  159.8 20.3 %copy-start.2 = (bf16[256,768]{1,0:T(8,128)(2,1)S(1)}, bf16[256,768]{1,0:T(8,128)(2,1)}, u32[]{:S(2)}) copy-start(bf16[256,768]{1,0:T(8,128)(2,1)} %get-tuple-element.69) | copy-start | bytes 1179652
  178.8 26.6 %collective-permute-start.8 = (bf16[256,768]{1,0:T(8,128)(2,1)}, bf16[256,768]{1,0:T(8,128)(2,1)S(1)}, u32[]{:S(2)}, u32[]{:S(2)}) collective-permute-start(bf16[256,768]{1,0:T(8,128)(2,1)} %get-tuple-element.81), channel_id=1, source_target_pairs={{16,0},{17,1},{18,2},{19,3},{20,4},{21,5},{22,6},{23,7},{24,8},{25... | collective-permute-start | bytes 1179656 | tf_op jit(solution)/shard_map/ppermute | solution.py:349
  180.2 11.2 %collective-permute-start.7 = (bf16[64,768]{1,0:T(8,128)(2,1)S(1)}, bf16[64,768]{1,0:T(8,128)(2,1)S(1)}, u32[]{:S(2)}, u32[]{:S(2)}) collective-permute-start(bf16[64,768]{1,0:T(8,128)(2,1)S(1)} %get-tuple-element.164), channel_id=1, source_target_pairs={{4,16},{8,20},{12,24},{5,17},{9,21},{13,25},{6,18},{10,22},{14,26}... | collective-permute-start | bytes 294920 | tf_op jit(solution)/shard_map/ppermute | solution.py:344
  180.8 11.7 %collective-permute-start.6 = (bf16[64,768]{1,0:T(8,128)(2,1)S(1)}, bf16[64,768]{1,0:T(8,128)(2,1)S(1)}, u32[]{:S(2)}, u32[]{:S(2)}) collective-permute-start(bf16[64,768]{1,0:T(8,128)(2,1)S(1)} %get-tuple-element.165), channel_id=1, source_target_pairs={{0,20},{4,24},{8,28},{1,21},{5,25},{9,29},{2,22},{6,26},{10,30},{3... | collective-permute-start | bytes 294920 | tf_op jit(solution)/shard_map/ppermute | solution.py:343
  190.0 15.4 %collective-permute-start.10 = (bf16[64,768]{1,0:T(8,128)(2,1)S(1)}, bf16[64,768]{1,0:T(8,128)(2,1)S(1)}, u32[]{:S(2)}, u32[]{:S(2)}) collective-permute-start(bf16[64,768]{1,0:T(8,128)(2,1)S(1)} %get-tuple-element.170), channel_id=1, source_target_pairs={{20,0},{24,4},{28,8},{21,1},{25,5},{29,9},{22,2},{26,6},{30,10},{2... | collective-permute-start | bytes 294920 | tf_op jit(solution)/shard_map/ppermute | solution.py:351
  191.3 14.1 %collective-permute-start.9 = (bf16[64,768]{1,0:T(8,128)(2,1)S(1)}, bf16[64,768]{1,0:T(8,128)(2,1)S(1)}, u32[]{:S(2)}, u32[]{:S(2)}) collective-permute-start(bf16[64,768]{1,0:T(8,128)(2,1)S(1)} %get-tuple-element.171), channel_id=1, source_target_pairs={{16,4},{20,8},{24,12},{17,5},{21,9},{25,13},{18,6},{22,10},{26,14}... | collective-permute-start | bytes 294920 | tf_op jit(solution)/shard_map/ppermute | solution.py:350
  225.6 15.4 %collective-permute-start.11 = (bf16[256,768]{1,0:T(8,128)(2,1)}, bf16[256,768]{1,0:T(8,128)(2,1)S(1)}, u32[]{:S(2)}, u32[]{:S(2)}) collective-permute-start(bf16[256,768]{1,0:T(8,128)(2,1)} %get-tuple-element.89), channel_id=1, source_target_pairs={{16,0},{17,1},{18,2},{19,3},{20,4},{21,5},{22,6},{23,7},{24,8},{25... | collective-permute-start | bytes 1179656 | tf_op jit(solution)/shard_map/ppermute | solution.py:349
  227.9 8.2 %collective-permute-start.13 = (bf16[64,768]{1,0:T(8,128)(2,1)S(1)}, bf16[64,768]{1,0:T(8,128)(2,1)S(1)}, u32[]{:S(2)}, u32[]{:S(2)}) collective-permute-start(bf16[64,768]{1,0:T(8,128)(2,1)S(1)} %get-tuple-element.168), channel_id=1, source_target_pairs={{20,0},{24,4},{28,8},{21,1},{25,5},{29,9},{22,2},{26,6},{30,10},{2... | collective-permute-start | bytes 294920 | tf_op jit(solution)/shard_map/ppermute | solution.py:351
  229.2 6.9 %collective-permute-start.12 = (bf16[64,768]{1,0:T(8,128)(2,1)S(1)}, bf16[64,768]{1,0:T(8,128)(2,1)S(1)}, u32[]{:S(2)}, u32[]{:S(2)}) collective-permute-start(bf16[64,768]{1,0:T(8,128)(2,1)S(1)} %get-tuple-element.169), channel_id=1, source_target_pairs={{16,4},{20,8},{24,12},{17,5},{21,9},{25,13},{18,6},{22,10},{26,14}... | collective-permute-start | bytes 294920 | tf_op jit(solution)/shard_map/ppermute | solution.py:350
  273.3 57.8 %reduce-scatter.14.cloned.1.call-start = ((), (), s32[]{:S(2)}) async-start(), calls=%async_computation.8 | async-start | bytes 2211840 | tf_op jit(solution)/shard_map/reduce_scatter | solution.py:368
  273.9 100.2 %reduce-scatter.8.cloned.1.call-start = ((), (), s32[]{:S(2)}) async-start(), calls=%async_computation.5 | async-start | bytes 4423680 | tf_op jit(solution)/shard_map/reduce_scatter | solution.py:368
  274.6 142.7 %reduce-scatter.12.cloned.1.call-start = ((), (), s32[]{:S(2)}) async-start(), calls=%async_computation.7 | async-start | bytes 4423680 | tf_op jit(solution)/shard_map/reduce_scatter | solution.py:368
  275.4 142.0 %copy-start.1 = (bf16[256,768]{1,0:T(8,128)(2,1)S(1)}, bf16[256,768]{1,0:T(8,128)(2,1)}, u32[]{:S(2)}) copy-start(bf16[256,768]{1,0:T(8,128)(2,1)} %get-tuple-element.68) | copy-start | bytes 1179652
  275.4 164.7 %reduce-scatter.16.cloned.1.call-start = ((), (), s32[]{:S(2)}) async-start(), calls=%async_computation.13 | async-start | bytes 245760
  276.4 267.8 %all-reduce.5.cloned.1.call-start = ((), (), s32[]{:S(2)}) async-start(), calls=%async_computation.14 | async-start | bytes 5013504 | tf_op jit(solution)/shard_map/psum | solution.py:370
  417.4 36.1 %copy-start.4 = (f32[256,768]{1,0:T(8,128)S(1)}, f32[256,768]{1,0:T(8,128)}, u32[]{:S(2)}) copy-start(f32[256,768]{1,0:T(8,128)} %get-tuple-element.92) | copy-start | bytes 2359300
  417.4 36.1 %copy-start.5 = (f32[256,768]{1,0:T(8,128)S(1)}, f32[256,768]{1,0:T(8,128)}, u32[]{:S(2)}) copy-start(f32[256,768]{1,0:T(8,128)} %get-tuple-element.88) | copy-start | bytes 2359300
  417.4 36.1 %copy-start.6 = (f32[256,768]{1,0:T(8,128)S(1)}, f32[256,768]{1,0:T(8,128)}, u32[]{:S(2)}) copy-start(f32[256,768]{1,0:T(8,128)} %get-tuple-element.91) | copy-start | bytes 2359300
  420.6 32.9 %collective-permute-start.14 = (bf16[2,64,768]{2,1,0:T(8,128)(2,1)S(1)}, bf16[2,64,768]{2,1,0:T(8,128)(2,1)S(1)}, u32[]{:S(2)}, u32[]{:S(2)}) collective-permute-start(bf16[2,64,768]{2,1,0:T(8,128)(2,1)S(1)} %get-tuple-element.162), channel_id=1, source_target_pairs={{0,4},{4,8},{8,12},{1,5},{5,9},{9,13},{2,6},{6,10},{10,14},{3,7},{... | collective-permute-start | bytes 589832 | tf_op jit(solution)/shard_map/ppermute | solution.py:364
  424.0 29.5 %collective-permute-start.15 = (bf16[2,64,768]{2,1,0:T(8,128)(2,1)S(1)}, bf16[2,64,768]{2,1,0:T(8,128)(2,1)S(1)}, u32[]{:S(2)}, u32[]{:S(2)}) collective-permute-start(bf16[2,64,768]{2,1,0:T(8,128)(2,1)S(1)} %get-tuple-element.163), channel_id=1, source_target_pairs={{4,0},{8,4},{12,8},{5,1},{9,5},{13,9},{6,2},{10,6},{14,10},{7,3},{... | collective-permute-start | bytes 589832 | tf_op jit(solution)/shard_map/ppermute | solution.py:365
  (25 other events, 61.6 us)
Sparse Core Ops, SparseCore 0:
  9.6 20.1 all-gather.11
  31.3 20.7 all-gather.15
  53.7 30.7 all-gather.9
  85.9 30.7 all-gather.13
  273.4 25.0 reduce-scatter.9
  301.7 29.3 reduce-scatter.13
  333.7 40.3 reduce-scatter.7
  376.9 40.4 reduce-scatter.11
  420.3 19.7 reduce-scatter.15
  442.6 101.5 all-reduce.4

commit v2 on v1

--- a/solution.py
+++ b/solution.py
@@ -269,12 +269,45 @@
     )(*args, *gains, *mats, *kept_a, *kept_b)
 
 
-def weight_kernel(*refs):
+PIECES = ((3, 0), (2, 0), (2, 1), (2, 2), (1, 0), (0, 0), (0, 1), (0, 2))
+MESH = pl.DeviceIdType.MESH
+
+
+def remote(src, dst, sems, p, i, axis, target):
+    return pltpu.make_async_remote_copy(
+        src_ref=src, dst_ref=dst, send_sem=sems.at[p, 2 * i], recv_sem=sems.at[p, 2 * i + 1],
+        device_id={axis: target}, device_id_type=MESH)
+
+
+def signal_to(axis, target):
+    pl.semaphore_signal(pltpu.get_barrier_semaphore(), inc=1, device_id={axis: target}, device_id_type=MESH)
+
+
+def weight_kernel(seq_count, *refs):
+    chain = seq_count == 4
     slots = (refs[0:8], refs[8:16], refs[16:24])
-    outs = refs[24:28]
-    bufs = refs[28:36]
-    sems = refs[36]
+    ln_terms = (refs[24:27], refs[27:30])
+    outs = refs[30:35]
+    bufs = refs[35:43]
+    full, from_core, from_y, from_l, from_r, total = (refs[43 + 9 * i:52 + 9 * i] for i in range(6))
+    sems, rsems = refs[97:99]
     sec = lax.axis_index("section")
+    f = lax.axis_index("fsdp")
+    z = lax.axis_index("seq")
+    core = lax.rem(f, 2)
+    y = f // 2
+    sibling = y * 2 + (1 - core)
+    across = (1 - y) * 2 + core
+    signal_to("fsdp", sibling)
+    signal_to("fsdp", across)
+    if chain:
+        @pl.when(z > 0)
+        def _():
+            signal_to("seq", z - 1)
+
+        @pl.when(z < seq_count - 1)
+        def _():
+            signal_to("seq", z + 1)
     order = (6, 7, 4, 5, 2, 3, 0, 1)
 
     def copy(slot, i, part):
@@ -293,28 +326,312 @@
         def _():
             copy(0, i, 1).start()
 
-    for w in (3, 2, 1, 0):
-        for i in (2 * w, 2 * w + 1):
-            copy(1, i, 0).wait()
-            copy(2, i, 1).wait()
-        left = bufs[2 * w][...]
-        width = outs[w].shape[1]
-        step = 384
-        for c in range(0, width, step):
-            outs[w][:, c:c + step] = dot_tn(left, bufs[2 * w + 1][:, c:c + step]).astype(BF)
-
-
-def weight_call(slots):
+    def core_copies(p):
+        return [remote(full[p].at[k * 2 + (1 - core)], from_core[p].at[k], rsems, p, k, "fsdp", sibling)
+                for k in range(2)]
+
+    def y_copy(p):
+        return remote(full[p].at[(1 - y) * 2 + core], from_y[p], rsems, p, 2, "fsdp", across)
+
+    def add_core(p):
+        for c in core_copies(p):
+            c.wait()
+        for k in range(2):
+            own = full[p].at[k * 2 + core]
+            own[...] = (own[...].astype(F32) + from_core[p][k].astype(F32)).astype(BF)
+        y_copy(p).start()
+
+    count = len(PIECES) + 1
+    ready = set()
+    for p in range(count):
+        if p < count - 1:
+            w, part = PIECES[p]
+            if w not in ready:
+                ready.add(w)
+                for i in (2 * w, 2 * w + 1):
+                    copy(1, i, 0).wait()
+                    copy(2, i, 1).wait()
+            prod = dot_tn(bufs[2 * w][...], bufs[2 * w + 1][:, part * D:part * D + D]).astype(BF)
+            rb = prod.shape[0] // 4
+            for k in range(4):
+                full[p][k] = prod[k * rb:(k + 1) * rb]
+        else:
+            both = [jnp.broadcast_to(t[0][...] + t[1][...] + t[2][...], (8, D)) for t in ln_terms]
+            both = jnp.concatenate(both, axis=0).astype(BF)
+            for k in range(4):
+                full[p][k] = both
+        if p == 0:
+            peers = 2
+            if chain:
+                peers = 2 + (z + seq_count - 1) // seq_count + (2 * seq_count - 2 - z) // seq_count
+            pl.semaphore_wait(pltpu.get_barrier_semaphore(), peers)
+        for c in core_copies(p):
+            c.start()
+        if p > 0:
+            add_core(p - 1)
+    add_core(count - 1)
+
+    def acc(p):
+        return full[p].at[y * 2 + core]
+
+    def store(p, ref):
+        if p < count - 1:
+            w, part = PIECES[p]
+            outs[w][:, part * D:part * D + D] = ref[...]
+        else:
+            outs[4][...] = ref[...]
+
+    def go_right(p):
+        return remote(acc(p), from_l[p], rsems, p, 3, "seq", z + 1)
+
+    def go_left(p):
+        return remote(acc(p), from_r[p], rsems, p, 4, "seq", z - 1)
+
+    def total_right(p):
+        return remote(total[p], total[p], rsems, p, 5, "seq", z + 1)
+
+    def total_left(p):
+        return remote(total[p], total[p], rsems, p, 6, "seq", z - 1)
+
+    def add_from(p, ref):
+        mine = acc(p)
+        mine[...] = (mine[...].astype(F32) + ref[...].astype(F32)).astype(BF)
+
+    def step_a(p):
+        y_copy(p).wait()
+        add_from(p, from_y[p])
+        if not chain:
+            store(p, acc(p))
+            return
+
+        @pl.when(z == 0)
+        def _():
+            go_right(p).start()
+
+        @pl.when(z == 3)
+        def _():
+            go_left(p).start()
+
+    def step_b(p):
+        @pl.when(z == 1)
+        def _():
+            remote(acc(p), from_l[p], rsems, p, 3, "seq", z - 1).wait_recv()
+            add_from(p, from_l[p])
+            if p % 2:
+                go_right(p).start()
+
+        @pl.when(z == 2)
+        def _():
+            remote(acc(p), from_r[p], rsems, p, 4, "seq", z + 1).wait_recv()
+            add_from(p, from_r[p])
+            if p % 2 == 0:
+                go_left(p).start()
+
+    def step_c(p):
+        if p % 2:
+            @pl.when(z == 2)
+            def _():
+                remote(acc(p), from_l[p], rsems, p, 3, "seq", z - 1).wait_recv()
+                add_from(p, from_l[p])
+                total[p][...] = acc(p)[...]
+                total_left(p).start()
+                total_right(p).start()
+                store(p, total[p])
+        else:
+            @pl.when(z == 1)
+            def _():
+                remote(acc(p), from_r[p], rsems, p, 4, "seq", z + 1).wait_recv()
+                add_from(p, from_r[p])
+                total[p][...] = acc(p)[...]
+                total_left(p).start()
+                total_right(p).start()
+                store(p, total[p])
+
+    def got_from_left(p):
+        remote(total[p], total[p], rsems, p, 5, "seq", z - 1).wait_recv()
+
+    def got_from_right(p):
+        remote(total[p], total[p], rsems, p, 6, "seq", z + 1).wait_recv()
+
+    def step_d(p):
+        if p % 2:
+            @pl.when(z == 1)
+            def _():
+                got_from_right(p)
+                total_left(p).start()
+                store(p, total[p])
+
+            @pl.when(z == 3)
+            def _():
+                got_from_left(p)
+                store(p, total[p])
+        else:
+            @pl.when(z == 2)
+            def _():
+                got_from_left(p)
+                total_right(p).start()
+                store(p, total[p])
+
+            @pl.when(z == 0)
+            def _():
+                got_from_right(p)
+                store(p, total[p])
+
+    def step_e(p):
+        if p % 2:
+            @pl.when(z == 0)
+            def _():
+                got_from_right(p)
+                store(p, total[p])
+        else:
+            @pl.when(z == 3)
+            def _():
+                got_from_left(p)
+                store(p, total[p])
+
+    steps = (step_a, step_b, step_c, step_d, step_e) if chain else (step_a,)
+    for t in range(count + len(steps) - 1):
+        for lag, step in enumerate(steps):
+            if 0 <= t - lag < count:
+                step(t - lag)
+    if not chain:
+        return
+    for p in range(count):
+        odd = p % 2
+
+        @pl.when(z == 0)
+        def _():
+            go_right(p).wait_send()
+
+        @pl.when(z == 3)
+        def _():
+            go_left(p).wait_send()
+
+        @pl.when(z == 1)
+        def _():
+            if odd:
+                go_right(p).wait_send()
+                total_left(p).wait_send()
+            else:
+                total_left(p).wait_send()
+                total_right(p).wait_send()
+
+        @pl.when(z == 2)
+        def _():
+            if odd:
+                total_left(p).wait_send()
+                total_right(p).wait_send()
+            else:
+                go_left(p).wait_send()
+                total_right(p).wait_send()
+
+
+def weight_call(slots, ln_terms, seq_count):
     shape = jax.ShapeDtypeStruct
+    blocks = [288 if w == 3 else 192 for w, _ in PIECES] + [16]
+    blocks[0] = FF // 4
     scratch = [pltpu.VMEM((2 * x.shape[0], x.shape[1]), BF) for x in slots[0]]
+    scratch += [pltpu.VMEM((4, rb, D), BF) for rb in blocks]
+    scratch += [pltpu.VMEM((2, rb, D), BF) for rb in blocks]
+    for _ in range(4):
+        scratch += [pltpu.VMEM((rb, D), BF) for rb in blocks]
     return pl.pallas_call(
-        weight_kernel,
-        out_shape=(shape((D, 3 * D), BF), shape((D, D), BF), shape((D, 2 * FF), BF), shape((FF, D), BF)),
-        in_specs=[ANY] * 24,
-        out_specs=(VM,) * 4,
-        scratch_shapes=scratch + [pltpu.SemaphoreType.DMA((2, 8))],
-        compiler_params=pltpu.CompilerParams(vmem_limit_bytes=VMEM_LIMIT),
-    )(*slots[0], *slots[1], *slots[2])
+        functools.partial(weight_kernel, seq_count),
+        out_shape=(shape((D // 4, 3 * D), BF), shape((D // 4, D), BF), shape((D // 4, 2 * FF), BF),
+                   shape((FF // 4, D), BF), shape((16, D), BF)),
+        in_specs=[ANY] * 24 + [VM] * 6,
+        out_specs=(VM,) * 5,
+        scratch_shapes=scratch + [pltpu.SemaphoreType.DMA((2, 8)), pltpu.SemaphoreType.DMA((9, 14))],
+        compiler_params=pltpu.CompilerParams(vmem_limit_bytes=VMEM_LIMIT, collective_id=1, has_side_effects=True),
+    )(*slots[0], *slots[1], *slots[2], *ln_terms)
+
+
+GATHER = ((0, 0), (0, 1), (0, 2), (1, 0), (2, 0), (2, 1), (2, 2), (3, 0))
+
+
+def gather_kernel(*refs):
+    ins, outs, sems, lsems = refs[0:5], refs[5:10], refs[10], refs[11]
+    f = lax.axis_index("fsdp")
+    z = lax.axis_index("seq")
+    core = lax.rem(f, 2)
+    y = f // 2
+    sibling = y * 2 + (1 - core)
+    across = (1 - y) * 2 + core
+    near = z + 1 - 2 * lax.rem(z, 2)
+    signal_to("fsdp", sibling)
+    signal_to("fsdp", across)
+    signal_to("seq", near)
+    count = len(GATHER) + 1
+
+    def own(p):
+        if p == 0:
+            return ins[4]
+        w, part = GATHER[p - 1]
+        return ins[w].at[:, pl.ds(part * D, D)]
+
+    def place(p, who):
+        if p == 0:
+            return outs[4].at[who]
+        w, part = GATHER[p - 1]
+        return outs[w].at[who, :, pl.ds(part * D, D)]
+
+    locals_ = [pltpu.make_async_copy(own(p), place(p, f), lsems.at[p]) for p in range(count)]
+    for c in locals_:
+        c.start()
+    pl.semaphore_wait(pltpu.get_barrier_semaphore(), 3)
+    for par in range(2):
+        @pl.when(lax.rem(z, 2) == par)
+        def _():
+            for p in range(par, count, 2):
+                remote(own(p), place(p, f), sems, p, 0, "fsdp", across).start()
+    for p in range(count):
+        remote(own(p), place(p, f), sems, p, 1, "fsdp", sibling).start()
+
+    def z_copy(p):
+        return remote(place(p, across), place(p, across), sems, p, 2, "seq", near)
+
+    def forward_copy(p):
+        return remote(place(p, across), place(p, across), sems, p, 3, "fsdp", sibling)
+
+    for par in range(2):
+        @pl.when(lax.rem(z, 2) == par)
+        def _():
+            mine = list(range(par, count, 2))
+            other = list(range(1 - par, count, 2))
+            for j in range(6):
+                if j < len(mine):
+                    p = mine[j]
+                    remote(own(p), place(p, across), sems, p, 0, "fsdp", across).wait_recv()
+                    z_copy(p).start()
+                    forward_copy(p).start()
+                if 1 <= j and j - 1 < len(other):
+                    p = other[j - 1]
+                    z_copy(p).wait_recv()
+                    forward_copy(p).start()
+            for p in mine:
+                remote(own(p), place(p, f), sems, p, 0, "fsdp", across).wait_send()
+                z_copy(p).wait_send()
+    for p in range(count):
+        locals_[p].wait()
+        first = remote(own(p), place(p, f), sems, p, 1, "fsdp", sibling)
+        first.wait_send()
+        remote(own(p), place(p, sibling), sems, p, 1, "fsdp", sibling).wait_recv()
+        forward_copy(p).wait_send()
+        opposite = (1 - y) * 2 + (1 - core)
+        remote(place(p, across), place(p, opposite), sems, p, 3, "fsdp", sibling).wait_recv()
+
+
+def gather_call(weights, gains):
+    shape = jax.ShapeDtypeStruct
+    args = tuple(weights) + (gains,)
+    return pl.pallas_call(
+        gather_kernel,
+        out_shape=tuple(shape((4,) + x.shape, BF) for x in args),
+        in_specs=[ANY] * 5,
+        out_specs=(ANY,) * 5,
+        scratch_shapes=[pltpu.SemaphoreType.DMA((9, 8)), pltpu.SemaphoreType.DMA((9,))],
+        compiler_params=pltpu.CompilerParams(collective_id=0, has_side_effects=True),
+    )(*args)
 
 
 def neighbours(seq_count, from_sec, to_sec, by):
@@ -333,9 +650,11 @@
     from_left = lax.ppermute(x[:, rows - HALF:], "seq", right)
     from_right = lax.ppermute(x[:, :HALF], "seq", left)
     own = jnp.concatenate([from_left, x, from_right], axis=1)
-    mats = tuple(lax.all_gather(w[0], "fsdp", axis=0, tiled=True) for w in (w_qkv, w_attn_out, w_in, w_ff_out))
-    gains = lax.all_gather(jnp.concatenate([ln_attn, ln_ff], axis=0), "fsdp", axis=1, tiled=True).astype(F32)
-    gains = (gains[0:1], gains[1:2])
+    lnb = jnp.concatenate([jnp.broadcast_to(ln_attn, (8, D // 4)), jnp.broadcast_to(ln_ff, (8, D // 4))], axis=0)
+    lnb = jnp.pad(lnb, ((0, 0), (0, 64)))
+    got = gather_call((w_qkv[0], w_attn_out[0], w_in[0], w_ff_out[0]), lnb)
+    mats = tuple(g.reshape(-1, g.shape[2]) for g in got[:4])
+    gains = (got[4][:, 0, :D // 4].astype(F32).reshape(1, D), got[4][:, 8, :D // 4].astype(F32).reshape(1, D))
 
     def relay(out):
         return (
@@ -363,12 +682,11 @@
     rims = jnp.where(sec == 0, jnp.stack([back1[2], back2[2]]), jnp.stack([back0[2], back1[2]]))
     to_right = lax.ppermute(rims[:, HALF:], "seq", right).astype(F32)
     to_left = lax.ppermute(rims[:, :HALF], "seq", left).astype(F32)
-    totals = weight_call([b[3:11] for b in backs])
-    ln_totals = jnp.concatenate([sum(b[11] for b in backs), sum(b[12] for b in backs)], axis=0)
-    owned = tuple(lax.psum_scatter(t, "fsdp", scatter_dimension=0, tiled=True) for t in totals)
-    owned_ln = lax.psum_scatter(ln_totals.astype(BF), "fsdp", scatter_dimension=1, tiled=True)
-    summed = lax.psum(owned + (owned_ln,), "seq")
+    summed = weight_call([b[3:11] for b in backs], [b[11] for b in backs] + [b[12] for b in backs], seq_count)
+    if seq_count != 4:
+        summed = lax.psum(tuple(summed), "seq")
     summed = tuple(s.astype(F32) for s in summed)
+    g_ln = lax.dynamic_slice_in_dim(summed[4], lax.axis_index("fsdp") * (D // 4), D // 4, axis=1)
     layer_out = jnp.where(sec == 0, jnp.stack([kept0[5], kept1[5]]), jnp.stack([kept1[5], kept2[5]]))
     grad = jnp.where(sec == 0, jnp.stack([back1[0], back2[0]]), jnp.stack([back0[0], back1[0]]))
     pad = ((0, 0), (0, rows - HALF), (0, 0))
@@ -376,7 +694,7 @@
     grad = grad + jnp.pad(to_left, (pad[0], pad[1][::-1], pad[2]))
     grad = jnp.where(sec == 1, grad.astype(BF).astype(F32), grad)
     return (layer_out[None, :, None], grad[None, :, None], summed[0][None], summed[1][None], summed[2][None],
-            summed[3][None], summed[4][0:1], summed[4][1:2])
+            summed[3][None], g_ln[0:1], g_ln[8:9])
 
 
 def solution(mesh):

time: 564 us -> 364 us (0.65)
  waiting for transfers between devices: 360 us -> 12.8 us
  Pallas kernels: 105 us -> 277 us
  blocking collectives: 17 us -> 0 us
  between operations: 15 us -> 1.3 us
    pallas_call x1 -> x2, Pallas kernels: 12.5 us -> 185 us  [the longest x1 107 us: weight_call(): pl.pallas_call(functools.partial(weight_kernel, seq_count), out_shape=(sh...]
    reduce_scatter x4 -> x0, waiting for transfers between devices: 141 us -> none  [body(): lax.psum_scatter(t, 'fsdp', scatter_dimension=0, tiled=True)]
    all_gather x4 -> x0, waiting for transfers between devices: 92.3 us -> none  [body(): lax.all_gather(w[0], 'fsdp', axis=0, tiled=True)]
    psum x1 -> x0, waiting for transfers between devices: 89.4 us -> none  [body(): summed = lax.psum(owned + (owned_ln,), 'seq')]
    unnamed x11 -> x0, waiting for transfers between devices: 19.3 us -> none
    psum x1 -> x0, blocking collectives: 11.9 us -> none  [body(): summed = lax.psum(owned + (owned_ln,), 'seq')]
  transfers between devices with their start and end apart: 26 -> 16, of which waited for: 15 -> 4; matrix products, arithmetic and copies ran while one was open for 2% -> 5% of each run, Pallas kernels for 5% -> 60%
where the time goes in v2:
time: 364 us; the launch traced here: 357 us
  Pallas kernels  277 us (76%)
  starting transfers between devices  41.5 us (11%)
  other arithmetic  12.9 us (4%)
  waiting for transfers between devices  12.8 us (4%)
  local copies, waits for them, and re-layouts  11.8 us (3%)
    pallas_call x1, Pallas kernels, weight_call(): pl.pallas_call(functools.partial(weight_kernel, seq_count), out_shape=(sh...  107 us
    pallas_call x1, Pallas kernels, gather_call(): pl.pallas_call(gather_kernel, out_shape=tuple((shape((4,) + x.shape, BF)...  78 us
    pallas_call x3, Pallas kernels, backward_call(): pl.pallas_call(functools.partial(backward_kernel, cot is not None, recv i...  57.6 us
    pallas_call x3, Pallas kernels, forward_call(): pl.pallas_call(functools.partial(forward_kernel, own is not None, recv is...  34.8 us
    ppermute x2, starting transfers between devices, relay(): lax.ppermute(out[rows - HALF:], axes, neighbours(seq_count, 0, 1, 1))  13.3 us
    ppermute x2, starting transfers between devices, relay(): lax.ppermute(out, 'section', [(0, 1)])  8.13 us
  transfers between devices with their start and end apart: 16, of which 4 were waited for; matrix products, arithmetic and copies ran while one was open for 5% of the time, Pallas kernels for 60%

profile of v2, /device:TPU:0, one launch (start us, length us, event | category | flops | bytes accessed | tf_op | source)
XLA Modules:
  0.0 357.3 jit_solution(14918929353698871935)
XLA Ops:
  0.6 1.1 fusion.5
  1.8 4.9 %collective-permute-start = (bf16[2,64,768]{2,1,0:T(8,128)(2,1)S(1)}, bf16[2,64,768]{2,1,0:T(8,128)(2,1)S(1)}, u32[]{:S(2)}, u32[]{:S(2)}) collective-permute-start(bf16[2,64,768]{2,1,0:T(8,128)(2,1)S(1)} %get-tuple-element.154), channel_id=1, source_target_pairs={{0,4},{4,8},{8,12},{1,5},{5,9},{9,13},{2,6},{6,10},{10,14},{3,7},{... | collective-permute-start | bytes 589832 | tf_op jit(solution)/shard_map/ppermute | solution.py:650
  6.7 1.3 collective-permute-start.1
  10.0 78.0 %shard_map.143 = (bf16[4,192,2304]{2,1,0:T(8,128)(2,1)}, bf16[4,192,768]{2,1,0:T(8,128)(2,1)}, bf16[4,192,2304]{2,1,0:T(8,128)(2,1)}, bf16[4,288,768]{2,1,0:T(8,128)(2,1)}, bf16[4,16,256]{2,1,0:T(8,128)(2,1)}) custom-call(bf16[192,2304]{1,0:T(8,128)(2,1)} %bitcast.68, bf16[192,768]{1,0:T(8,128)(2,1)} %bitcast.79, bf16[192,2304]{1,0:T(8,128)(2,1)} %bitcast.69, ...), custom_call_target="tpu_custom_call" | custom-call | tf_op jit(solution)/shard_map/pallas_call | solution.py:627
  90.3 1.1 slice_bitcast_fusion.1
  91.4 11.6 %shard_map.144 = (bf16[384,768]{1,0:T(8,128)(2,1)}, bf16[384,2304]{1,0:T(8,128)(2,1)}, bf16[256,768]{1,0:T(8,128)(2,1)}, f32[256,768]{1,0:T(8,128)}, f32[256,2304]{1,0:T(8,128)}, /*index=5*/bf16[256,768]{1,0:T(8,128)(2,1)}) custom-call(bf16[384,768]{1,0:T(8,128)(2,1)} %get-tuple-element.150.refs_0_, f32[1,768]{1,0:T(1,128)} %reshape.121.refs_1_.refs_4_.refs_3_, ...), custom_call_target="tpu_custom_call" | custom-call | tf_op jit(solution)/shard_map/pallas_call | solution.py:136
  102.9 3.4 collective-permute-start.2
  108.0 4.2 %collective-permute-start.3 = (bf16[64,768]{1,0:T(8,128)(2,1)S(1)}, bf16[64,768]{1,0:T(8,128)(2,1)S(1)}, u32[]{:S(2)}, u32[]{:S(2)}) collective-permute-start(bf16[64,768]{1,0:T(8,128)(2,1)S(1)} %get-tuple-element.161), channel_id=1, source_target_pairs={{0,20},{4,24},{8,28},{1,21},{5,25},{9,29},{2,22},{6,26},{10,30},{3... | collective-permute-start | bytes 294920 | tf_op jit(solution)/shard_map/ppermute | solution.py:662
  113.2 1.3 collective-permute-done.3.refs_2_
  114.5 2.3 collective-permute-done.2.refs_1_
  117.6 11.7 %shard_map.145 = (bf16[384,768]{1,0:T(8,128)(2,1)}, bf16[384,2304]{1,0:T(8,128)(2,1)}, bf16[256,768]{1,0:T(8,128)(2,1)}, f32[256,768]{1,0:T(8,128)}, f32[256,2304]{1,0:T(8,128)}, /*index=5*/bf16[256,768]{1,0:T(8,128)(2,1)}) custom-call(bf16[384,768]{1,0:T(8,128)(2,1)} %get-tuple-element.151.refs_0_, bf16[256,768]{1,0:T(8,128)(2,1)} %copy-done.12, ...), custom_call_target="tpu_custom_call" | custom-call | tf_op jit(solution)/shard_map/pallas_call | solution.py:136
  129.3 4.7 %collective-permute-start.5 = (bf16[256,768]{1,0:T(8,128)(2,1)}, bf16[256,768]{1,0:T(8,128)(2,1)S(1)}, u32[]{:S(2)}, u32[]{:S(2)}) collective-permute-start(bf16[256,768]{1,0:T(8,128)(2,1)} %get-tuple-element.80), channel_id=1, source_target_pairs={{0,16},{1,17},{2,18},{3,19},{4,20},{5,21},{6,22},{7,23},{8,24},{9,... | collective-permute-start | bytes 1179656 | tf_op jit(solution)/shard_map/ppermute | solution.py:661
  134.1 18.9 %shard_map.147 = (f32[256,768]{1,0:T(8,128)}, bf16[256,768]{1,0:T(8,128)(2,1)}, bf16[128,768]{1,0:T(8,128)(2,1)}, bf16[384,768]{1,0:T(8,128)(2,1)}, bf16[384,230...) custom-call(bf16[256,768]{1,0:T(8,128)(2,1)} %get-tuple-element.152., ...), custom_call_target="tpu_custom_call" | custom-call | tf_op jit(solution)/shard_map/pallas_call | solution.py:255
  153.0 1.3 collective-permute-start.8
  155.0 9.1 %collective-permute-start.6 = (bf16[64,768]{1,0:T(8,128)(2,1)S(1)}, bf16[64,768]{1,0:T(8,128)(2,1)S(1)}, u32[]{:S(2)}, u32[]{:S(2)}) collective-permute-start(bf16[64,768]{1,0:T(8,128)(2,1)S(1)} %get-tuple-element.159), channel_id=1, source_target_pairs={{0,20},{4,24},{8,28},{1,21},{5,25},{9,29},{2,22},{6,26},{10,30},{3... | collective-permute-start | bytes 294920 | tf_op jit(solution)/shard_map/ppermute | solution.py:662
  165.1 1.3 collective-permute-start.10
  168.7 11.5 %shard_map.146 = (bf16[384,768]{1,0:T(8,128)(2,1)}, bf16[384,2304]{1,0:T(8,128)(2,1)}, bf16[256,768]{1,0:T(8,128)(2,1)}, f32[256,768]{1,0:T(8,128)}, f32[256,2304]{1,0:T(8,128)}, /*index=5*/bf16[256,768]{1,0:T(8,128)(2,1)}) custom-call(bf16[256,768]{1,0:T(8,128)(2,1)} %copy-done.11, bf16[64,768]{1,0:T(8,128)(2,1)} %copy-done.21, bf16[64,768]{1,0:T(8,128)(2,1)} %copy-done.20, ...), custom_call_target="tpu_custom_call" | custom-call | tf_op jit(solution)/shard_map/pallas_call | solution.py:136
  181.1 19.7 %shard_map.148 = (f32[256,768]{1,0:T(8,128)}, bf16[256,768]{1,0:T(8,128)(2,1)}, bf16[128,768]{1,0:T(8,128)(2,1)}, bf16[384,768]{1,0:T(8,128)(2,1)}, bf16[384,230...) custom-call(bf16[256,768]{1,0:T(8,128)(2,1)} %get-tuple-element.153., ...), custom_call_target="tpu_custom_call" | custom-call | tf_op jit(solution)/shard_map/pallas_call | solution.py:255
  200.7 1.3 collective-permute-start.11
  203.0 1.3 collective-permute-start.13
  205.0 1.0 maximum_select_fusion.1
  206.0 5.3 %collective-permute-done.13.refs_2_ = bf16[64,768]{1,0:T(8,128)(2,1)S(1)} collective-permute-done((bf16[64,768]{1,0:T(8,128)(2,1)S(1)}, bf16[64,768]{1,0:T(8,128)(2,1)S(1)}, u32[]{:S(2)}, u32[]{:S(2)}) %collective-permute-start.13) | collective-permute-done | bytes 98336 | tf_op jit(solution)/shard_map/ppermute | solution.py:670
  211.3 3.8 %collective-permute-done.11.refs_0_ = bf16[256,768]{1,0:T(8,128)(2,1)S(1)} collective-permute-done((bf16[256,768]{1,0:T(8,128)(2,1)}, bf16[256,768]{1,0:T(8,128)(2,1)S(1)}, u32[]{:S(2)}, u32[]{:S(2)}) %collective-permute-start.11) | collective-permute-done | bytes 393248 | tf_op jit(solution)/shard_map/ppermute | solution.py:668
  215.9 19.0 %shard_map.149 = (f32[256,768]{1,0:T(8,128)}, bf16[256,768]{1,0:T(8,128)(2,1)}, bf16[128,768]{1,0:T(8,128)(2,1)}, bf16[384,768]{1,0:T(8,128)(2,1)}, bf16[384,230...) custom-call(bf16[256,768]{1,0:T(8,128)(2,1)} %copy-done.14, ...), custom_call_target="tpu_custom_call" | custom-call | tf_op jit(solution)/shard_map/pallas_call | solution.py:255
  234.9 1.0 maximum_select_fusion.2
  235.9 4.6 %collective-permute-start.14 = (bf16[2,64,768]{2,1,0:T(8,128)(2,1)S(1)}, bf16[2,64,768]{2,1,0:T(8,128)(2,1)S(1)}, u32[]{:S(2)}, u32[]{:S(2)}) collective-permute-start(bf16[2,64,768]{2,1,0:T(8,128)(2,1)S(1)} %get-tuple-element.156), channel_id=1, source_target_pairs={{0,4},{4,8},{8,12},{1,5},{5,9},{9,13},{2,6},{6,10},{10,14},{3,7},{... | collective-permute-start | bytes 589832 | tf_op jit(solution)/shard_map/ppermute | solution.py:683
  240.5 1.3 collective-permute-start.15
  241.8 106.5 %shard_map.150 = (bf16[192,2304]{1,0:T(8,128)(2,1)}, bf16[192,768]{1,0:T(8,128)(2,1)}, bf16[192,2304]{1,0:T(8,128)(2,1)}, bf16[288,768]{1,0:T(8,128)(2,1)}, bf16[16,768]{1,0:T(8,128)(2,1)}) custom-call(bf16[384,768]{1,0:T(8,128)(2,1)} %get-tuple-element.105.refs_0_, bf16[384,2304]{1,0:T(8,128)(2,1)} %get-tuple-element.106.refs_1_, ...), custom_call_target="tpu_custom_call" | custom-call | tf_op jit(solution)/shard_map/pallas_call | solution.py:538
  348.4 1.9 bitcast_convert_fusion.3
  350.3 2.0 bitcast_convert_fusion.2
  353.1 2.0 bitcast_convert_fusion
  355.8 1.3 select_bitcast_fusion
  (81 shorter events, 16.1 us)
Async XLA Ops:
  0.6 89.6 %copy-start = (bf16[2,1,256,768]{3,2,1,0:T(8,128)(2,1)S(1)}, bf16[2,1,256,768]{3,2,1,0:T(8,128)(2,1)}, u32[]{:S(2)}) copy-start(bf16[2,1,256,768]{3,2,1,0:T(8,128)(2,1)} %param.8) | copy-start | bytes 2359300
  1.8 88.4 %collective-permute-start = (bf16[2,64,768]{2,1,0:T(8,128)(2,1)S(1)}, bf16[2,64,768]{2,1,0:T(8,128)(2,1)S(1)}, u32[]{:S(2)}, u32[]{:S(2)}) collective-permute-start(bf16[2,64,768]{2,1,0:T(8,128)(2,1)S(1)} %get-tuple-element.154), channel_id=1, source_target_pairs={{0,4},{4,8},{8,12},{1,5},{5,9},{9,13},{2,6},{6,10},{10,14},{3,7},{... | collective-permute-start | bytes 589832 | tf_op jit(solution)/shard_map/ppermute | solution.py:650
  6.7 83.5 %collective-permute-start.1 = (bf16[2,64,768]{2,1,0:T(8,128)(2,1)S(1)}, bf16[2,64,768]{2,1,0:T(8,128)(2,1)S(1)}, u32[]{:S(2)}, u32[]{:S(2)}) collective-permute-start(bf16[2,64,768]{2,1,0:T(8,128)(2,1)S(1)} %get-tuple-element.155), channel_id=1, source_target_pairs={{4,0},{8,4},{12,8},{5,1},{9,5},{13,9},{6,2},{10,6},{14,10},{7,3},{... | collective-permute-start | bytes 589832 | tf_op jit(solution)/shard_map/ppermute | solution.py:651
  91.4 20.8 %copy-start.10 = (bf16[2,1,256,768]{3,2,1,0:T(8,128)(2,1)S(1)}, bf16[2,1,256,768]{3,2,1,0:T(8,128)(2,1)}, u32[]{:S(2)}) copy-start(bf16[2,1,256,768]{3,2,1,0:T(8,128)(2,1)} %param.9) | copy-start | bytes 2359300
  102.9 13.9 %collective-permute-start.2 = (bf16[256,768]{1,0:T(8,128)(2,1)}, bf16[256,768]{1,0:T(8,128)(2,1)S(1)}, u32[]{:S(2)}, u32[]{:S(2)}) collective-permute-start(bf16[256,768]{1,0:T(8,128)(2,1)} %get-tuple-element.79), channel_id=1, source_target_pairs={{0,16},{1,17},{2,18},{3,19},{4,20},{5,21},{6,22},{7,23},{8,24},{9,... | collective-permute-start | bytes 1179656 | tf_op jit(solution)/shard_map/ppermute | solution.py:661
  107.3 5.9 %collective-permute-start.4 = (bf16[64,768]{1,0:T(8,128)(2,1)S(1)}, bf16[64,768]{1,0:T(8,128)(2,1)S(1)}, u32[]{:S(2)}, u32[]{:S(2)}) collective-permute-start(bf16[64,768]{1,0:T(8,128)(2,1)S(1)} %get-tuple-element.160), channel_id=1, source_target_pairs={{4,16},{8,20},{12,24},{5,17},{9,21},{13,25},{6,18},{10,22},{14,26}... | collective-permute-start | bytes 294920 | tf_op jit(solution)/shard_map/ppermute | solution.py:663
  108.0 6.5 %collective-permute-start.3 = (bf16[64,768]{1,0:T(8,128)(2,1)S(1)}, bf16[64,768]{1,0:T(8,128)(2,1)S(1)}, u32[]{:S(2)}, u32[]{:S(2)}) collective-permute-start(bf16[64,768]{1,0:T(8,128)(2,1)S(1)} %get-tuple-element.161), channel_id=1, source_target_pairs={{0,20},{4,24},{8,28},{1,21},{5,25},{9,29},{2,22},{6,26},{10,30},{3... | collective-permute-start | bytes 294920 | tf_op jit(solution)/shard_map/ppermute | solution.py:662
  113.2 3.6 %copy-start.22 = (bf16[64,768]{1,0:T(8,128)(2,1)}, bf16[64,768]{1,0:T(8,128)(2,1)S(1)}, u32[]{:S(2)}) copy-start(bf16[64,768]{1,0:T(8,128)(2,1)S(1)} %collective-permute-done.4.refs_3_) | copy-start | bytes 294916
  114.5 2.3 copy-start.23
  129.3 38.0 %collective-permute-start.5 = (bf16[256,768]{1,0:T(8,128)(2,1)}, bf16[256,768]{1,0:T(8,128)(2,1)S(1)}, u32[]{:S(2)}, u32[]{:S(2)}) collective-permute-start(bf16[256,768]{1,0:T(8,128)(2,1)} %get-tuple-element.80), channel_id=1, source_target_pairs={{0,16},{1,17},{2,18},{3,19},{4,20},{5,21},{6,22},{7,23},{8,24},{9,... | collective-permute-start | bytes 1179656 | tf_op jit(solution)/shard_map/ppermute | solution.py:661
  134.0 20.3 %copy-start.2 = (bf16[256,768]{1,0:T(8,128)(2,1)S(1)}, bf16[256,768]{1,0:T(8,128)(2,1)}, u32[]{:S(2)}) copy-start(bf16[256,768]{1,0:T(8,128)(2,1)} %get-tuple-element.80) | copy-start | bytes 1179652
  153.0 27.3 %collective-permute-start.8 = (bf16[256,768]{1,0:T(8,128)(2,1)}, bf16[256,768]{1,0:T(8,128)(2,1)S(1)}, u32[]{:S(2)}, u32[]{:S(2)}) collective-permute-start(bf16[256,768]{1,0:T(8,128)(2,1)} %get-tuple-element.92), channel_id=1, source_target_pairs={{16,0},{17,1},{18,2},{19,3},{20,4},{21,5},{22,6},{23,7},{24,8},{25... | collective-permute-start | bytes 1179656 | tf_op jit(solution)/shard_map/ppermute | solution.py:668
  154.3 12.1 %collective-permute-start.7 = (bf16[64,768]{1,0:T(8,128)(2,1)S(1)}, bf16[64,768]{1,0:T(8,128)(2,1)S(1)}, u32[]{:S(2)}, u32[]{:S(2)}) collective-permute-start(bf16[64,768]{1,0:T(8,128)(2,1)S(1)} %get-tuple-element.158), channel_id=1, source_target_pairs={{4,16},{8,20},{12,24},{5,17},{9,21},{13,25},{6,18},{10,22},{14,26}... | collective-permute-start | bytes 294920 | tf_op jit(solution)/shard_map/ppermute | solution.py:663
  155.0 12.2 %collective-permute-start.6 = (bf16[64,768]{1,0:T(8,128)(2,1)S(1)}, bf16[64,768]{1,0:T(8,128)(2,1)S(1)}, u32[]{:S(2)}, u32[]{:S(2)}) collective-permute-start(bf16[64,768]{1,0:T(8,128)(2,1)S(1)} %get-tuple-element.159), channel_id=1, source_target_pairs={{0,20},{4,24},{8,28},{1,21},{5,25},{9,29},{2,22},{6,26},{10,30},{3... | collective-permute-start | bytes 294920 | tf_op jit(solution)/shard_map/ppermute | solution.py:662
  165.1 15.1 %collective-permute-start.10 = (bf16[64,768]{1,0:T(8,128)(2,1)S(1)}, bf16[64,768]{1,0:T(8,128)(2,1)S(1)}, u32[]{:S(2)}, u32[]{:S(2)}) collective-permute-start(bf16[64,768]{1,0:T(8,128)(2,1)S(1)} %get-tuple-element.164), channel_id=1, source_target_pairs={{20,0},{24,4},{28,8},{21,1},{25,5},{29,9},{22,2},{26,6},{30,10},{2... | collective-permute-start | bytes 294920 | tf_op jit(solution)/shard_map/ppermute | solution.py:670
  166.4 13.8 %collective-permute-start.9 = (bf16[64,768]{1,0:T(8,128)(2,1)S(1)}, bf16[64,768]{1,0:T(8,128)(2,1)S(1)}, u32[]{:S(2)}, u32[]{:S(2)}) collective-permute-start(bf16[64,768]{1,0:T(8,128)(2,1)S(1)} %get-tuple-element.165), channel_id=1, source_target_pairs={{16,4},{20,8},{24,12},{17,5},{21,9},{25,13},{18,6},{22,10},{26,14}... | collective-permute-start | bytes 294920 | tf_op jit(solution)/shard_map/ppermute | solution.py:669
  181.1 23.9 %copy-start.1 = (bf16[256,768]{1,0:T(8,128)(2,1)S(1)}, bf16[256,768]{1,0:T(8,128)(2,1)}, u32[]{:S(2)}) copy-start(bf16[256,768]{1,0:T(8,128)(2,1)} %get-tuple-element.79) | copy-start | bytes 1179652
  181.1 23.9 %copy-start.13 = (bf16[256,768]{1,0:T(8,128)(2,1)S(1)}, bf16[256,768]{1,0:T(8,128)(2,1)}, u32[]{:S(2)}) copy-start(bf16[256,768]{1,0:T(8,128)(2,1)} %get-tuple-element.81) | copy-start | bytes 1179652
  200.7 14.4 %collective-permute-start.11 = (bf16[256,768]{1,0:T(8,128)(2,1)}, bf16[256,768]{1,0:T(8,128)(2,1)S(1)}, u32[]{:S(2)}, u32[]{:S(2)}) collective-permute-start(bf16[256,768]{1,0:T(8,128)(2,1)} %get-tuple-element.100), channel_id=1, source_target_pairs={{16,0},{17,1},{18,2},{19,3},{20,4},{21,5},{22,6},{23,7},{24,8},{25... | collective-permute-start | bytes 1179656 | tf_op jit(solution)/shard_map/ppermute | solution.py:668
  203.0 8.3 %collective-permute-start.13 = (bf16[64,768]{1,0:T(8,128)(2,1)S(1)}, bf16[64,768]{1,0:T(8,128)(2,1)S(1)}, u32[]{:S(2)}, u32[]{:S(2)}) collective-permute-start(bf16[64,768]{1,0:T(8,128)(2,1)S(1)} %get-tuple-element.162), channel_id=1, source_target_pairs={{20,0},{24,4},{28,8},{21,1},{25,5},{29,9},{22,2},{26,6},{30,10},{2... | collective-permute-start | bytes 294920 | tf_op jit(solution)/shard_map/ppermute | solution.py:670
  204.3 7.0 %collective-permute-start.12 = (bf16[64,768]{1,0:T(8,128)(2,1)S(1)}, bf16[64,768]{1,0:T(8,128)(2,1)S(1)}, u32[]{:S(2)}, u32[]{:S(2)}) collective-permute-start(bf16[64,768]{1,0:T(8,128)(2,1)S(1)} %get-tuple-element.163), channel_id=1, source_target_pairs={{16,4},{20,8},{24,12},{17,5},{21,9},{25,13},{18,6},{22,10},{26,14}... | collective-permute-start | bytes 294920 | tf_op jit(solution)/shard_map/ppermute | solution.py:669
  206.0 28.9 %copy-start.8 = (bf16[128,768]{1,0:T(8,128)(2,1)S(1)}, bf16[128,768]{1,0:T(8,128)(2,1)}, u32[]{:S(2)}) copy-start(bf16[128,768]{1,0:T(8,128)(2,1)} %get-tuple-element.93) | copy-start | bytes 589828
  206.0 28.9 %copy-start.9 = (bf16[128,768]{1,0:T(8,128)(2,1)S(1)}, bf16[128,768]{1,0:T(8,128)(2,1)}, u32[]{:S(2)}) copy-start(bf16[128,768]{1,0:T(8,128)(2,1)} %get-tuple-element.101) | copy-start | bytes 589828
  211.3 3.8 %copy-start.17 = (bf16[64,768]{1,0:T(8,128)(2,1)}, bf16[64,768]{1,0:T(8,128)(2,1)S(1)}, u32[]{:S(2)}) copy-start(bf16[64,768]{1,0:T(8,128)(2,1)S(1)} %collective-permute-done.13.refs_2_) | copy-start | bytes 294916
  211.3 3.8 %copy-start.19 = (bf16[64,768]{1,0:T(8,128)(2,1)}, bf16[64,768]{1,0:T(8,128)(2,1)S(1)}, u32[]{:S(2)}) copy-start(bf16[64,768]{1,0:T(8,128)(2,1)S(1)} %collective-permute-done.12.refs_1_) | copy-start | bytes 294916
  235.9 119.8 %collective-permute-start.14 = (bf16[2,64,768]{2,1,0:T(8,128)(2,1)S(1)}, bf16[2,64,768]{2,1,0:T(8,128)(2,1)S(1)}, u32[]{:S(2)}, u32[]{:S(2)}) collective-permute-start(bf16[2,64,768]{2,1,0:T(8,128)(2,1)S(1)} %get-tuple-element.156), channel_id=1, source_target_pairs={{0,4},{4,8},{8,12},{1,5},{5,9},{9,13},{2,6},{6,10},{10,14},{3,7},{... | collective-permute-start | bytes 589832 | tf_op jit(solution)/shard_map/ppermute | solution.py:683
  240.5 115.2 %collective-permute-start.15 = (bf16[2,64,768]{2,1,0:T(8,128)(2,1)S(1)}, bf16[2,64,768]{2,1,0:T(8,128)(2,1)S(1)}, u32[]{:S(2)}, u32[]{:S(2)}) collective-permute-start(bf16[2,64,768]{2,1,0:T(8,128)(2,1)S(1)} %get-tuple-element.157), channel_id=1, source_target_pairs={{4,0},{8,4},{12,8},{5,1},{9,5},{13,9},{6,2},{10,6},{14,10},{7,3},{... | collective-permute-start | bytes 589832 | tf_op jit(solution)/shard_map/ppermute | solution.py:684
  348.3 4.7 %copy-start.3 = (bf16[192,2304]{1,0:T(8,128)(2,1)S(1)}, bf16[192,2304]{1,0:T(8,128)(2,1)}, u32[]{:S(2)}) copy-start(bf16[192,2304]{1,0:T(8,128)(2,1)} %get-tuple-element.135) | copy-start | bytes 2654212
  348.3 4.7 %copy-start.4 = (bf16[192,2304]{1,0:T(8,128)(2,1)S(1)}, bf16[192,2304]{1,0:T(8,128)(2,1)}, u32[]{:S(2)}) copy-start(bf16[192,2304]{1,0:T(8,128)(2,1)} %get-tuple-element.137) | copy-start | bytes 2654212
  353.1 2.6 copy-start.5
  353.1 2.6 copy-start.6
  353.1 2.7 copy-start.7
  (8 other events, 5.9 us)
